TPU v7x, 512 devices: a whole 4x8x8 slice. The times are simulated.
512 devices in a mesh: dp: 4 (over y_lo), seq: 64 (over x, z, core), tensor: 2 (over y_hi).
Axes of the slice: x: 4, y: 8 (y_hi: 2, y_lo: 4; y = y_hi * 4 + y_lo), z: 8, core: 2. Of those that a mesh axis runs over, the one named last changes fastest.
Arguments:
- img_query: bfloat16 [64, 512, 1280], P('seq', 'dp', 'tensor'), may hold values from -8 to 8
- img_key: bfloat16 [64, 512, 1280], P('seq', 'dp', 'tensor'), may hold values from -8 to 8
- img_value: bfloat16 [64, 512, 1280], P('seq', 'dp', 'tensor'), may hold values from -6 to 6
- txt_query: bfloat16 [64, 128, 1280], P('seq', None, 'tensor'), may hold values from -8 to 8
- txt_key: bfloat16 [64, 128, 1280], P('seq', None, 'tensor'), may hold values from -8 to 8
- txt_value: bfloat16 [64, 128, 1280], P('seq', None, 'tensor'), may hold values from -6 to 6
- img_cotangent: bfloat16 [64, 512, 1280], P('seq', 'dp', 'tensor'), may hold values from -6 to 6
- txt_cotangent: bfloat16 [64, 128, 1280], P('seq', None, 'tensor'), may hold values from -6 to 6
- norm_gains: float32 [4, 64], replicated, may hold values from 1 to 3
Outputs:
- img_out: bfloat16 [64, 512, 1280], P('seq', 'dp', 'tensor')
- txt_out: bfloat16 [64, 128, 1280], P('seq', None, 'tensor')
- img_grads: bfloat16 [3, 64, 512, 1280], P(None, 'seq', 'dp', 'tensor')
- txt_grads: bfloat16 [3, 64, 128, 1280], P(None, 'seq', None, 'tensor')
- gain_grads: float32 [4, 64], replicated
All inputs are finite; a program needn't handle non-finite values.
Results may differ from a plain program's by a relative error of at most 0.02.
Values may be sent and summed in bfloat16 or wider, within the bound.
A program may use at most 64 MiB of HBM per device.

v0:
```python
import jax
import jax.numpy as jnp
from jax import lax
from jax.sharding import PartitionSpec as P

HEAD_DIM = 64


epsilon = 1e-06


def norm_forward(flattened, gain_row):
    values = flattened.astype(jnp.float32).reshape(flattened.shape[0], -1, HEAD_DIM)
    inverse = lax.rsqrt(jnp.mean(values * values, axis=-1, keepdims=True) + epsilon)
    unit_rows = values * inverse
    return (unit_rows, inverse, (unit_rows * gain_row).astype(jnp.bfloat16))


def norm_backward(gradient, unit_rows, inverse, gain_row):
    weighted = gradient * gain_row
    inner = jnp.mean(weighted * unit_rows, axis=-1, keepdims=True)
    result = (inverse * (weighted - unit_rows * inner)).astype(jnp.bfloat16)
    return (result, jnp.sum(gradient * unit_rows, axis=(0, 1)))


def scores_of(queries, keys_in):
    return jnp.einsum(
        "qhd,khd->hqk", queries, keys_in, preferred_element_type=jnp.float32
    ) * HEAD_DIM ** (-0.5)


def weigh_values(weights, values_in):
    return jnp.einsum("hqk,khd->qhd", weights, values_in, preferred_element_type=jnp.float32)


def weigh_queries(weights, queries):
    return jnp.einsum("hqk,qhd->khd", weights, queries, preferred_element_type=jnp.float32)


def score_grads(scores, logtotal, deltas, cotangent, values_in):
    probability = jnp.exp(scores - logtotal[:, :, None])
    grad_prob = jnp.einsum("qhd,khd->hqk", cotangent, values_in, preferred_element_type=jnp.float32)
    grad_score = (probability * (grad_prob - deltas[:, :, None])).astype(jnp.bfloat16)
    return (probability.astype(jnp.bfloat16), grad_score)


def local(
    img_query,
    img_key,
    img_value,
    txt_query,
    txt_key,
    txt_value,
    img_cotangent,
    txt_cotangent,
    norm_gains,
):
    tok_rows = img_query.shape[1]
    txt_rows = txt_query.shape[1]
    row_width = img_query.shape[2]
    head_count = row_width // HEAD_DIM
    factor = HEAD_DIM ** (-0.5)
    cycle_count = lax.axis_size("dp")
    first_cycle = (lax.axis_index("dp") == 0).astype(jnp.float32)
    unit_iq, inv_iq, normed_iq = norm_forward(img_query[0], norm_gains[0])
    unit_ik, inv_ik, normed_ik = norm_forward(img_key[0], norm_gains[1])
    unit_tq, inv_tq, normed_tq = norm_forward(txt_query[0], norm_gains[2])
    unit_tk, inv_tk, normed_tk = norm_forward(txt_key[0], norm_gains[3])
    img_values = img_value[0].reshape(tok_rows, head_count, HEAD_DIM)
    txt_values = txt_value[0].reshape(txt_rows, head_count, HEAD_DIM)
    img_cots = img_cotangent[0].reshape(tok_rows, head_count, HEAD_DIM)
    txt_cots = txt_cotangent[0].reshape(txt_rows, head_count, HEAD_DIM)
    flat_ik = normed_ik.reshape(tok_rows, row_width)
    flat_iq = normed_iq.reshape(tok_rows, row_width)
    all_keys, all_values = (
        lax.all_gather(flat_ik, "dp", axis=0, tiled=True),
        lax.all_gather(img_value[0], "dp", axis=0, tiled=True),
    )
    img_total = all_keys.shape[0]
    joint_keys = jnp.concatenate(
        [all_keys.reshape(img_total, head_count, HEAD_DIM), normed_tk], axis=0
    )
    joint_values = jnp.concatenate(
        [all_values.reshape(img_total, head_count, HEAD_DIM), txt_values], axis=0
    )
    local_rows = normed_iq.shape[0]
    local_scores = scores_of(normed_iq, joint_keys)
    local_exp = jnp.exp(local_scores)
    local_total = jnp.sum(local_exp, axis=-1)
    local_log = jnp.log(local_total)
    local_num = weigh_values(local_exp.astype(jnp.bfloat16), joint_values)
    local_out = (local_num / local_total.T[:, :, None]).astype(jnp.bfloat16)
    delta_rows = jnp.sum(img_cots.astype(jnp.float32) * local_out.astype(jnp.float32), axis=-1)
    local_deltas = delta_rows.T
    stats_log, stats_delta = (
        lax.all_gather(local_log.T, "dp", axis=0, tiled=True),
        lax.all_gather(delta_rows, "dp", axis=0, tiled=True),
    )
    stats_log = stats_log.reshape(cycle_count, local_rows, head_count)
    stats_delta = stats_delta.reshape(cycle_count, local_rows, head_count)
    img_log = stats_log.reshape(img_total, head_count).T
    img_delta = stats_delta.reshape(img_total, head_count).T
    side_exp = jnp.exp(scores_of(normed_tq, normed_ik))
    part_num = weigh_values(side_exp.astype(jnp.bfloat16), img_values).reshape(txt_rows, row_width)
    sum_num, sum_total = lax.psum((part_num, jnp.sum(side_exp, axis=-1)), "dp")
    self_scores = scores_of(normed_tq, normed_tk)
    self_exp = jnp.exp(self_scores)
    txt_total = sum_total + jnp.sum(self_exp, axis=-1)
    txt_num = sum_num.reshape(txt_rows, head_count, HEAD_DIM) + weigh_values(
        self_exp.astype(jnp.bfloat16), txt_values
    )
    txt_out = (txt_num / txt_total.T[:, :, None]).astype(jnp.bfloat16)
    txt_log = jnp.log(txt_total)
    txt_delta = jnp.sum(txt_cots.astype(jnp.float32) * txt_out.astype(jnp.float32), axis=-1).T
    all_queries, all_cots = (
        lax.all_gather(flat_iq, "dp", axis=0, tiled=True),
        lax.all_gather(img_cotangent[0], "dp", axis=0, tiled=True),
    )
    local_prob, local_ds = score_grads(
        local_scores, local_log, local_deltas, img_cots, joint_values
    )
    local_dq = weigh_values(local_ds, joint_keys) * factor
    part_dk = weigh_queries(local_ds[:, :, img_total:], normed_iq) * factor
    part_dv = weigh_queries(local_prob[:, :, img_total:], img_cots)
    every_q = jnp.concatenate(
        [all_queries.reshape(img_total, head_count, HEAD_DIM), normed_tq], axis=0
    )
    every_cots = jnp.concatenate(
        [all_cots.reshape(img_total, head_count, HEAD_DIM), txt_cots], axis=0
    )
    every_log = jnp.concatenate([img_log, txt_log], axis=1)
    every_delta = jnp.concatenate([img_delta, txt_delta], axis=1)
    key_scores = scores_of(every_q, normed_ik)
    key_prob, key_ds = score_grads(key_scores, every_log, every_delta, every_cots, img_values)
    grad_iv = weigh_queries(key_prob, every_cots)
    grad_key_rows = weigh_queries(key_ds, every_q) * factor
    side_dq = weigh_values(key_ds[:, img_total:], normed_ik) * factor
    self_prob, self_ds = score_grads(self_scores, txt_log, txt_delta, txt_cots, txt_values)
    sum_dq, sum_dk, sum_dv = (
        lax.psum(side_dq.reshape(txt_rows, row_width).astype(jnp.bfloat16), "dp").astype(
            jnp.float32
        ),
        lax.psum(part_dk.reshape(txt_rows, row_width).astype(jnp.bfloat16), "dp").astype(
            jnp.float32
        ),
        lax.psum(part_dv.reshape(txt_rows, row_width).astype(jnp.bfloat16), "dp").astype(
            jnp.float32
        ),
    )
    txt_dq = (
        sum_dq.reshape(txt_rows, head_count, HEAD_DIM) + weigh_values(self_ds, normed_tk) * factor
    )
    txt_dk = (
        sum_dk.reshape(txt_rows, head_count, HEAD_DIM) + weigh_queries(self_ds, normed_tq) * factor
    )
    txt_dv = sum_dv.reshape(txt_rows, head_count, HEAD_DIM) + weigh_queries(self_prob, txt_cots)
    full_grad, gain_tq = norm_backward(txt_dq, unit_tq, inv_tq, norm_gains[2])
    grad_tq = full_grad.reshape(txt_rows, row_width)
    gain_tq = gain_tq * first_cycle
    grad_tk, gain_tk = norm_backward(txt_dk, unit_tk, inv_tk, norm_gains[3])
    grad_iq, gain_iq = norm_backward(local_dq, unit_iq, inv_iq, norm_gains[0])
    grad_ik, gain_ik = norm_backward(grad_key_rows, unit_ik, inv_ik, norm_gains[1])
    gain_grads = lax.psum(
        jnp.stack([gain_iq, gain_ik, gain_tq, gain_tk * first_cycle]), ("dp", "seq", "tensor")
    )
    img_out = local_out.reshape(1, tok_rows, row_width)
    txt_result = txt_out.reshape(1, txt_rows, row_width)
    img_grads = jnp.stack(
        [
            grad_iq.reshape(tok_rows, row_width),
            grad_ik.reshape(tok_rows, row_width),
            grad_iv.astype(jnp.bfloat16).reshape(tok_rows, row_width),
        ]
    )[:, None]
    txt_grads = jnp.stack(
        [
            grad_tq,
            grad_tk.reshape(txt_rows, row_width),
            txt_dv.astype(jnp.bfloat16).reshape(txt_rows, row_width),
        ]
    )[:, None]
    return (img_out, txt_result, img_grads, txt_grads, gain_grads)


def solution(mesh):
    in_specs = (
        P("seq", "dp", "tensor"),
        P("seq", "dp", "tensor"),
        P("seq", "dp", "tensor"),
        P("seq", None, "tensor"),
        P("seq", None, "tensor"),
        P("seq", None, "tensor"),
        P("seq", "dp", "tensor"),
        P("seq", None, "tensor"),
        P(),
    )
    out_specs = (
        P("seq", "dp", "tensor"),
        P("seq", None, "tensor"),
        P(None, "seq", "dp", "tensor"),
        P(None, "seq", None, "tensor"),
        P(),
    )
    return jax.shard_map(local, mesh=mesh, in_specs=in_specs, out_specs=out_specs, check_vma=False)
```

profile of v0, /device:TPU:1, one launch (start us, length us, event | category | flops | bytes accessed | tf_op | source)
XLA Modules:
  0.0 335.8 jit_solution(1824256558977995929)
XLA Ops:
  13.3 15.5 %all-gather = bf16[1,512,640]{2,1,0:T(8,128)(2,1)S(1)} all-gather(bf16[1,128,640]{2,1,0:T(8,128)(2,1)S(1)} %copy-done.31), channel_id=2, replica_groups=mesh['dp'=4,'seq'=64,'tensor'=2] {'dp'}, dimensions={1}, use_global_device_ids=true | all-gather | bytes 819200 | tf_op jit(solution)/shard_map/all_gather | solution.py:77
  29.6 16.0 %all-gather.1 = bf16[1,512,640]{2,1,0:T(8,128)(2,1)S(1)} all-gather(bf16[1,128,640]{2,1,0:T(8,128)(2,1)S(1)} %copy-done.32), channel_id=3, replica_groups=mesh['dp'=4,'seq'=64,'tensor'=2] {'dp'}, dimensions={1}, use_global_device_ids=true | all-gather | bytes 819200 | tf_op jit(solution)/shard_map/all_gather | solution.py:117
  46.7 14.2 %all_gather.19 = bf16[512,640]{1,0:T(8,128)(2,1)S(1)} all-gather(bf16[128,640]{1,0:T(8,128)(2,1)S(1)} %fusion.50), channel_id=1, replica_groups=mesh['dp'=4,'seq'=64,'tensor'=2] {'dp'}, dimensions={0}, use_global_device_ids=true | all-gather | bytes 819200 | tf_op jit(solution)/shard_map/all_gather | solution.py:76
  63.8 2.5 exponential_reduce_fusion
  68.2 1.7 copy.60
  69.9 9.7 %psum.43 = f32[10,128]{1,0:T(8,128)S(1)} all-reduce(f32[10,128]{1,0:T(8,128)S(1)} %get-tuple-element.36), channel_id=1, replica_groups=mesh['dp'=4,'seq'=64,'tensor'=2] {'dp'}, use_global_device_ids=true, to_apply=%region_7.0 | all-reduce | flops 1280 | bytes 10240 | tf_op jit(solution)/shard_map/psum | solution.py:105
  80.0 12.4 %all_gather.20 = bf16[512,640]{1,0:T(8,128)(2,1)S(1)} all-gather(bf16[128,640]{1,0:T(8,128)(2,1)S(1)} %fusion.45), channel_id=1, replica_groups=mesh['dp'=4,'seq'=64,'tensor'=2] {'dp'}, dimensions={0}, use_global_device_ids=true | all-gather | bytes 819200 | tf_op jit(solution)/shard_map/all_gather | solution.py:116
  92.6 2.4 fusion.33
  95.0 10.3 %all_gather.21 = f32[512,10]{0,1:T(8,128)S(1)} all-gather(f32[128,10]{0,1:T(8,128)S(1)} %bitcast_log_fusion), channel_id=1, replica_groups=mesh['dp'=4,'seq'=64,'tensor'=2] {'dp'}, dimensions={0}, use_global_device_ids=true | all-gather | bytes 25600 | tf_op jit(solution)/shard_map/all_gather | solution.py:96
  106.5 2.6 subtract_exponential_fusion.1
  109.6 1.5 multiply_reduce_fusion.5
  113.4 2.2 fusion.40
  116.2 2.0 fusion.25
  118.8 1.7 copy.71
  120.5 1.7 copy.63
  122.3 10.6 %all_gather.23 = f32[512,10]{0,1:T(8,128)S(1)} all-gather(f32[128,10]{0,1:T(8,128)} %copy-done.39), channel_id=1, replica_groups=mesh['dp'=4,'seq'=64,'tensor'=2] {'dp'}, dimensions={0}, use_global_device_ids=true | all-gather | bytes 25600 | tf_op jit(solution)/shard_map/all_gather | solution.py:97
  132.9 1.8 fusion.28
  134.7 1.5 multiply_reduce_fusion.4
  136.8 4.1 %multiply_convert_fusion = bf16[10,640,128]{2,1,0:T(8,128)(2,1)S(1)} fusion(f32[10,640,128]{2,1,0:T(8,128)} %fusion.33, bf16[128,10,64]{0,2,1:T(8,128)(2,1)} %bitcast.194, f32[10,640]{1,0:T(8,128)S(1)} %pad_maximum_fusion.13, f32[10,640]{1,0:T(8,128)S(1)} %pad_maximum_fusion.12, bf16[128,10,64]{0,2,1:T(8,128)(2,1)} %bitcast.184, ...), kind=kOutput, calls=%fused_computation.2 | convolution fusion | flops 110592000 | bytes 5949440 | tf_op jit(solution)/shard_map/qhd,khd->hqk/dot_general | solution.py:42
  143.2 2.8 fusion.39
  149.7 73.6 %all-reduce.6.cloned.1.call-done = (bf16[128,10,64]{0,2,1:T(8,128)(2,1)}, bf16[128,10,64]{0,2,1:T(8,128)(2,1)}, bf16[128,10,64]{0,2,1:T(8,128)(2,1)}) async-done(((bf16[128,10,64]{0,2,1:T(8,128)(2,1)}, bf16[128,10,64]{0,2,1:T(8,128)(2,1)}, bf16[128,10,64]{0,2,1:T(8,128)(2,1)}), (bf16[128,10,64]{0,2,1:T(8,128)(2,1)}, bf16[128,10,64]{0,2,1:T(8,128)(2,1)}, ...) | async-done | bytes 491536 | tf_op jit(solution)/shard_map/psum | solution.py:146
  224.7 1.4 multiply_reduce_fusion
  226.1 1.3 multiply_reduce_fusion.1
  228.0 100.2 %psum.47 = f32[4,64]{1,0:T(4,128)} all-reduce(f32[4,64]{1,0:T(4,128)S(1)} %pad_maximum_fusion.14), channel_id=1, replica_groups=mesh['dp'=4,'seq'=64,'tensor'=2] {'dp','seq','tensor'}, use_global_device_ids=true, to_apply=%region_22.0 | all-reduce | flops 256 | bytes 2048 | tf_op jit(solution)/shard_map/psum | solution.py:163
  (174 shorter events, 27.4 us)
Async XLA Ops:
  7.2 21.6 %copy-start.32 = (bf16[1,128,640]{2,1,0:T(8,128)(2,1)S(1)}, bf16[1,128,640]{2,1,0:T(8,128)(2,1)}, u32[]{:S(2)}) copy-start(bf16[1,128,640]{2,1,0:T(8,128)(2,1)} %param.15) | copy-start | bytes 491524
  7.2 127.5 %all-reduce.4.cloned.1.call-start = ((), (), s32[]{:S(2)}) async-start(), calls=%async_computation | async-start | bytes 655360 | tf_op jit(solution)/shard_map/psum | solution.py:105
  8.1 54.4 %copy-start.45 = (f32[64]{0:T(128)}, f32[64]{0:T(128)S(1)}, u32[]{:S(2)}) copy-start(f32[64]{0:T(128)S(1)} %get-tuple-element.33) | copy-start | bytes 772
  9.1 36.5 %copy-start.9 = (f32[1,128,640]{1,2,0:T(8,128)}, f32[1,128,640]{1,2,0:T(8,128)S(1)}, u32[]{:S(2)}) copy-start(f32[1,128,640]{1,2,0:T(8,128)S(1)} %copy.47) | copy-start | bytes 983044
  9.1 36.5 %copy-start.47 = (f32[4,64]{1,0:T(4,128)S(1)}, f32[4,64]{1,0:T(4,128)}, u32[]{:S(2)}) copy-start(f32[4,64]{1,0:T(4,128)} %param.17) | copy-start | bytes 3076
  9.1 37.0 %copy-start.37 = (bf16[1,128,640]{2,1,0:T(8,128)(2,1)S(1)}, bf16[1,128,640]{2,1,0:T(8,128)(2,1)}, u32[]{:S(2)}) copy-start(bf16[1,128,640]{2,1,0:T(8,128)(2,1)} %param.13) | copy-start | bytes 491524
  10.4 36.0 %copy-start.4 = (f32[1,128,640]{1,2,0:T(8,128)}, f32[1,128,640]{1,2,0:T(8,128)S(1)}, u32[]{:S(2)}) copy-start(f32[1,128,640]{1,2,0:T(8,128)S(1)} %copy.51) | copy-start | bytes 983044
  11.6 35.0 %copy-start.29 = (bf16[1,128,640]{2,1,0:T(8,128)(2,1)S(1)}, bf16[1,128,640]{2,1,0:T(8,128)(2,1)}, u32[]{:S(2)}) copy-start(bf16[1,128,640]{2,1,0:T(8,128)(2,1)} %param.10) | copy-start | bytes 491524
  13.2 210.1 %all-reduce.6.cloned.1.call-start = ((), (), s32[]{:S(2)}) async-start(), calls=%async_computation.1 | async-start | bytes 983040 | tf_op jit(solution)/shard_map/psum | solution.py:146
  46.1 67.3 %copy-start.48 = (f32[64]{0:T(128)}, f32[64]{0:T(128)S(1)}, u32[]{:S(2)}) copy-start(f32[64]{0:T(128)S(1)} %get-tuple-element.28) | copy-start | bytes 772
  46.2 20.0 %copy-start.6 = (f32[1,128,640]{1,2,0:T(8,128)}, f32[1,128,640]{1,2,0:T(8,128)S(1)}, u32[]{:S(2)}) copy-start(f32[1,128,640]{1,2,0:T(8,128)S(1)} %copy.50) | copy-start | bytes 983044
  63.8 16.1 %copy-start.30 = (bf16[1,128,640]{2,1,0:T(8,128)(2,1)S(1)}, bf16[1,128,640]{2,1,0:T(8,128)(2,1)}, u32[]{:S(2)}) copy-start(bf16[1,128,640]{2,1,0:T(8,128)(2,1)} %param.9) | copy-start | bytes 491524
  66.3 26.4 %copy-start.21 = (bf16[128,10,64]{0,2,1:T(8,128)(2,1)S(1)}, bf16[128,10,64]{0,2,1:T(8,128)(2,1)}, u32[]{:S(2)}) copy-start(bf16[128,10,64]{0,2,1:T(8,128)(2,1)} %copy-done.20) | copy-start | bytes 491524
  92.6 13.8 %copy-start.17 = (bf16[512,640]{0,1:T(8,128)(2,1)}, bf16[512,640]{0,1:T(8,128)(2,1)S(1)}, u32[]{:S(2)}) copy-start(bf16[512,640]{0,1:T(8,128)(2,1)S(1)} %copy.58) | copy-start | bytes 1966084
  136.8 6.3 %copy-start.10 = (f32[1,128,640]{1,2,0:T(8,128)S(1)}, f32[1,128,640]{1,2,0:T(8,128)}, u32[]{:S(2)}) copy-start(f32[1,128,640]{1,2,0:T(8,128)} %copy-done.9) | copy-start | bytes 983044
  136.8 6.3 %copy-start.18 = (bf16[512,640]{0,1:T(8,128)(2,1)S(1)}, bf16[512,640]{0,1:T(8,128)(2,1)}, u32[]{:S(2)}) copy-start(bf16[512,640]{0,1:T(8,128)(2,1)} %copy-done.17) | copy-start | bytes 1966084
  136.8 6.3 %copy-start.50 = (f32[64]{0:T(128)S(1)}, f32[64]{0:T(128)}, u32[]{:S(2)}) copy-start(f32[64]{0:T(128)} %get-tuple-element.29) | copy-start | bytes 772
  143.1 6.2 %copy-start.8 = (f32[10,128,128]{1,2,0:T(8,128)S(1)}, f32[10,128,128]{1,2,0:T(8,128)}, u32[]{:S(2)}) copy-start(f32[10,128,128]{1,2,0:T(8,128)} %get-tuple-element.39) | copy-start | bytes 1966084
  146.0 78.7 %copy-start.7 = (f32[1,128,640]{1,2,0:T(8,128)S(1)}, f32[1,128,640]{1,2,0:T(8,128)}, u32[]{:S(2)}) copy-start(f32[1,128,640]{1,2,0:T(8,128)} %copy-done.6) | copy-start | bytes 983044
  146.0 78.7 %copy-start.46 = (f32[64]{0:T(128)S(1)}, f32[64]{0:T(128)}, u32[]{:S(2)}) copy-start(f32[64]{0:T(128)} %copy-done.45) | copy-start | bytes 772
  147.3 78.8 %copy-start.5 = (f32[1,128,640]{1,2,0:T(8,128)S(1)}, f32[1,128,640]{1,2,0:T(8,128)}, u32[]{:S(2)}) copy-start(f32[1,128,640]{1,2,0:T(8,128)} %copy-done.4) | copy-start | bytes 983044
  147.3 78.8 %copy-start.14 = (bf16[128,10,64]{0,2,1:T(8,128)(2,1)S(1)}, bf16[128,10,64]{0,2,1:T(8,128)(2,1)}, u32[]{:S(2)}) copy-start(bf16[128,10,64]{0,2,1:T(8,128)(2,1)} %copy-done.12) | copy-start | bytes 491524
  147.3 78.8 %copy-start.44 = (f32[64]{0:T(128)S(1)}, f32[64]{0:T(128)}, u32[]{:S(2)}) copy-start(f32[64]{0:T(128)} %copy-done.43) | copy-start | bytes 772
  149.6 78.3 %copy-start.52 = (f32[64]{0:T(128)S(1)}, f32[64]{0:T(128)}, u32[]{:S(2)}) copy-start(f32[64]{0:T(128)} %get-tuple-element.15) | copy-start | bytes 772
  (31 other events, 112.2 us)
Sparse Core Ops, SparseCore 0:
  13.3 60.8 all-reduce.3
  146.1 77.0 all-reduce.5
where the time goes:
time: 336 us
  blocking collectives  189 us (56%)
  waiting for transfers between devices  73.6 us (22%)
  matrix products  30 us (9%)
  local copies, waits for them, and re-layouts  20.3 us (6%)
  between operations  14.8 us (4%)
  other arithmetic  7.96 us (2%)
    psum x1, blocking collectives, local(): lax.psum(jnp.stack([gain_iq, gain_ik, gain_tq, gain_tk * first_cycle]), (...  100 us
    psum x1, waiting for transfers between devices, local(): lax.psum(part_dv.reshape(txt_rows, row_width).astype(jnp.bfloat16), 'dp')  73.6 us
    all_gather x1, blocking collectives, local(): lax.all_gather(img_cotangent[0], 'dp', axis=0, tiled=True)  16 us
    all_gather x1, blocking collectives, local(): lax.all_gather(img_value[0], 'dp', axis=0, tiled=True)  15.5 us
    all_gather x1, blocking collectives, local(): lax.all_gather(flat_ik, 'dp', axis=0, tiled=True)  14.2 us
    all_gather x1, blocking collectives, local(): lax.all_gather(flat_iq, 'dp', axis=0, tiled=True)  12.4 us
    all_gather x1, blocking collectives, local(): lax.all_gather(delta_rows, 'dp', axis=0, tiled=True)  10.6 us
    all_gather x1, blocking collectives, local(): lax.all_gather(local_log.T, 'dp', axis=0, tiled=True)  10.3 us
  transfers between devices with their start and end apart: 2, of which 1 were waited for; matrix products, arithmetic and copies ran while one was open for 10% of the time, Pallas kernels for 0%

commit v1 on v0

v1 whole, which is shorter than its diff:
```python
import jax
import jax.numpy as jnp
from jax import lax
from jax.experimental import pallas as pl
from jax.experimental.pallas import tpu as pltpu
from jax.sharding import PartitionSpec as P

HEAD_DIM = 64
EPSILON = 1e-6
ROWS = 128
LANES = 128
BLOCKS = 5
TEXT = 4 * ROWS
LOG2E = 1.4426950408889634
MESH = pl.DeviceIdType.MESH
NT = (((1,), (1,)), ((), ()))
f32, bf16 = jnp.float32, jnp.bfloat16


def dot(a, b):
    return jnp.dot(a, b, preferred_element_type=f32)


def dot_nt(a, b):
    return lax.dot_general(a, b, NT, preferred_element_type=f32)


def first_head():
    return lax.broadcasted_iota(jnp.int32, (ROWS, LANES), 1) < HEAD_DIM


def same_head():
    row = lax.broadcasted_iota(jnp.int32, (2 * LANES, LANES), 0)
    lane = lax.broadcasted_iota(jnp.int32, (2 * LANES, LANES), 1)
    return jnp.where(lax.rem(row, LANES) // HEAD_DIM == lane // HEAD_DIM, 1.0, 0.0).astype(bf16)


def identity():
    row = lax.broadcasted_iota(jnp.int32, (LANES, LANES), 0)
    lane = lax.broadcasted_iota(jnp.int32, (LANES, LANES), 1)
    return jnp.where(row == lane, 1.0, 0.0).astype(bf16)


def head_mean(z, same):
    high = z.astype(bf16)
    low = (z - high.astype(f32)).astype(bf16)
    return dot(jnp.concatenate([high, low], axis=1), same) * (1.0 / HEAD_DIM)


def norm(x, same):
    r = lax.rsqrt(head_mean(x * x, same) + EPSILON)
    return x * r, r


def norm_back(y, u, r, gain, same):
    w = y * gain
    return (r * (w - u * head_mean(w * u, same))).astype(bf16)


def by_head(x, first):
    zero = jnp.zeros_like(x)
    return jnp.concatenate([jnp.where(first, x, zero), jnp.where(first, zero, x)], axis=0)


def own_blocks(x):
    return jnp.concatenate([x[:HEAD_DIM, :ROWS], x[HEAD_DIM:, ROWS:]], axis=0)


def prepare_keys(rows, ins, gain, nk, uk, rk):
    u, r = norm(ins[1, rows, :].astype(f32), same_head())
    uk[rows, :] = u
    rk[rows, :] = r
    nk[rows, :] = (u * gain).astype(bf16)


def query_block(first_block, rows, ins, gain, nk, kt, vt, dk, dv, outs):
    same, first, eye = same_head(), first_head(), identity()
    u, r = norm(ins[0, rows, :].astype(f32), same)
    q = by_head((u * gain).astype(bf16), first)
    cot = ins[3, rows, :]
    g = by_head(cot, first)
    s = dot_nt(nk[...], q)
    e = jnp.exp2(s * (LOG2E * HEAD_DIM**-0.5))
    total = jnp.sum(e, axis=0, keepdims=True)
    p = e * (1.0 / total)
    pb = p.astype(bf16)
    out_t = own_blocks(dot(vt[...], pb)).astype(bf16)
    outs[0, rows, :] = dot_nt(eye, out_t).astype(bf16)
    z = out_t.astype(f32) * dot_nt(eye, cot)
    delta = jnp.concatenate(
        [
            jnp.sum(z[:HEAD_DIM], axis=0, keepdims=True),
            jnp.sum(z[HEAD_DIM:], axis=0, keepdims=True),
        ],
        axis=1,
    )
    ds = (p * (dot_nt(ins[2], g) - delta)).astype(bf16)
    new_dk, new_dv = dot(ds, q), dot(pb, g)
    if first_block:
        dk[...] = new_dk
        dv[...] = new_dv
    else:
        dk[...] += new_dk
        dv[...] += new_dv
    y = jnp.transpose(own_blocks(dot(kt[...], ds))) * HEAD_DIM**-0.5
    outs[1, rows, :] = norm_back(y, u, r, gain, same)
    return jnp.sum(y * u, axis=0, keepdims=True)


def key_block(rows, gain, dk, dv, uk, rk, outs):
    y = dk[rows, :] * HEAD_DIM**-0.5
    u, r = uk[rows, :], rk[rows, :]
    outs[2, rows, :] = norm_back(y, u, r, gain, same_head())
    outs[3, rows, :] = dv[rows, :].astype(bf16)
    return jnp.sum(y * u, axis=0, keepdims=True)


def kernel(
    iq, ik, iv, tq, tk, tv, ig, tg, gains_ref,
    img_out, txt_out, img_grads, txt_grads, gain_out,
    inb, outb, nk, uk, rk, kt, vt, dk, dv, gacc, racc, rbuf,
    in_local, in_send, in_recv, out_send, out_recv,
    txt_local, txt_send, txt_recv, gate_send, gate_recv, pass_send,
    red_send, red_recv,
):
    me = lax.axis_index("dp")
    seq = lax.axis_index("seq")
    tensor = lax.axis_index("tensor")
    core, z, x = lax.rem(seq, 2), lax.rem(seq // 2, 8), seq // 16
    y = tensor * 4 + me
    side = me // 2
    partner = me + 1 - 2 * lax.rem(me, 2)
    far_gate = 2 - side
    is_gate = jnp.logical_or(me == 1, me == 2)
    extra = 3 * core
    images = (iq, ik, iv, ig)
    texts = (tq, tk, tv, tg)

    def columns(owner):
        return pl.ds(pl.multiple_of(owner * LANES, LANES), LANES)

    def block(index):
        return pl.ds(pl.multiple_of(index * ROWS, ROWS), ROWS)

    def peer(i):
        return lax.rem(me + i, 4)

    def source(i):
        return lax.rem(me + 4 - i, 4)

    def dp(index):
        return (index, seq, tensor)

    def remote(src, dst, send, recv, to):
        return pltpu.make_async_remote_copy(
            src_ref=src, dst_ref=dst, send_sem=send, recv_sem=recv, device_id=to, device_id_type=MESH
        )

    def load(t, a, part):
        owner = me if t == 0 else 4
        src = (images if part == 0 else texts)[a].at[0, :, columns(owner)]
        rows = block(me) if part == 0 else pl.ds(TEXT, ROWS)
        return pltpu.make_async_copy(src, inb.at[t, a, rows], in_local.at[t, a, part])

    for a in (1, 2, 0, 3):
        for part in (1, 0):
            load(0, a, part).start()

    @pl.when(me == extra)
    def _():
        for a in (1, 2, 0, 3):
            for part in (1, 0):
                load(1, a, part).start()

    stages = (
        [
            (me, (lax.rem(x + i, 4) * 8 + z) * 2 + lax.rem(core + j, 2), tensor)
            for i in range(4)
            for j in range(2)
            if i or j
        ],
        [(me, (x * 8 + lax.rem(z + i, 8)) * 2 + core, tensor) for i in range(1, 8)],
        [(lax.rem(y + i, 4), seq, lax.rem(y + i, 8) // 4) for i in range(1, 8)],
    )

    barrier = pltpu.get_barrier_semaphore()
    for stage in stages:
        for to in stage:
            pl.semaphore_signal(barrier, inc=1, device_id=to, device_id_type=MESH)
    pl.semaphore_wait(barrier, sum(len(stage) for stage in stages))

    def hand(a, i):
        to = peer(i)
        return remote(
            images[a].at[0, :, columns(to)], inb.at[0, a, block(me)],
            in_send.at[0, a, i], in_recv.at[0, a, i], dp(to),
        )

    extra_way = lax.rem(extra + 4 - me, 4)

    def hand_extra(a):
        return remote(
            images[a].at[0, :, columns(4)], inb.at[1, a, block(me)],
            in_send.at[1, a, 0], in_recv.at[1, a, extra_way], dp(extra),
        )

    for pair in ((1, 2), (0, 3)):
        for i in (2, 3, 1):
            for a in pair:
                hand(a, i).start()

    @pl.when(me != extra)
    def _():
        for a in (1, 2, 0, 3):
            hand_extra(a).start()

    def await_rows(t, a, j):
        if j == 0 or j == 1:
            part = 1 - j
            rows = pl.ds(TEXT, ROWS) if j == 0 else block(me)
            pltpu.make_async_copy(
                texts[a].at[0, :, columns(0)], inb.at[t, a, rows], in_local.at[t, a, part]
            ).wait()
        else:
            i = j - 1
            rows = inb.at[t, a, block(source(i))]
            remote(rows, rows, in_send.at[t, a, i], in_recv.at[t, a, i], dp(source(i))).wait_recv()

    def result(t, group, rows):
        return outb.at[t, pl.ds(2, 2), rows] if group == 2 else outb.at[t, group, rows]

    def place(refs, group, owner):
        if group == 0:
            return refs[0].at[0, :, columns(owner)]
        if group == 1:
            return refs[1].at[0, 0, :, columns(owner)]
        return refs[1].at[pl.ds(1, 2), 0, :, columns(owner)]

    img_refs, txt_refs = (img_out, img_grads), (txt_out, txt_grads)

    def owner_of(t):
        return jnp.where(t == 0, me, 4)

    def keep(t, group):
        return pltpu.make_async_copy(
            result(t, group, block(me)), place(img_refs, group, owner_of(t)), out_send.at[t, group, 0]
        )

    def give(t, group, i):
        to = peer(i)
        return remote(
            result(t, group, block(to)), place(img_refs, group, owner_of(t)),
            out_send.at[t, group, i], out_recv.at[t, group, i], dp(to),
        )

    def text_copies(t, group):
        rows = result(t, group, pl.ds(TEXT, ROWS))
        spot = place(txt_refs, group, owner_of(t))
        slot = jnp.where(t == 0, lax.rem(me, 2), 2)
        return (
            remote(rows, spot, gate_send.at[t, group], gate_recv.at[slot, group], dp(far_gate)),
            remote(rows, spot, txt_send.at[t, group], txt_recv.at[t, group], dp(partner)),
            pltpu.make_async_copy(rows, spot, txt_local.at[t, group]),
        )

    gain = [jnp.concatenate([gains_ref[k : k + 1, :]] * 2, axis=1) for k in range(4)]
    gacc[...] = jnp.zeros_like(gacc)

    def do_tile(t, carry):
        ins, outs = inb.at[t], outb.at[t]

        def rows_of(j):
            return pl.ds(TEXT, ROWS) if j == 0 else block(me) if j == 1 else block(source(j - 1))

        def send(j, group):
            if j == 0:
                for c in text_copies(t, group):
                    c.start()
            elif j == 1:
                keep(t, group).start()
            else:
                give(t, group, 5 - j).start()

        for j in range(BLOCKS):
            await_rows(t, 1, j)
            prepare_keys(rows_of(j), ins, gain[3 if j == 0 else 1], nk, uk, rk)
        for j in range(BLOCKS):
            await_rows(t, 2, j)
        eye = identity()
        kt[...] = dot_nt(eye, nk[...]).astype(bf16)
        vt[...] = dot_nt(eye, ins[2]).astype(bf16)
        parts = []
        for j in range(BLOCKS):
            await_rows(t, 0, j)
            await_rows(t, 3, j)
            parts.append(
                query_block(j == 0, rows_of(j), ins, gain[2 if j == 0 else 0], nk, kt, vt, dk, dv, outs)
            )
            send(j, 0)
            send(j, 1)
        key_parts = []
        for j in range(BLOCKS):
            key_parts.append(
                key_block(rows_of(j), gain[3 if j == 0 else 1], dk, dv, uk, rk, outs)
            )
            send(j, 2)
        gacc[...] += jnp.concatenate(
            [sum(parts[1:]), sum(key_parts[1:]), parts[0], key_parts[0]], axis=0
        )
        return carry

    lax.fori_loop(0, jnp.where(me == extra, 2, 1), do_tile, 0)

    def cross(slot, group):
        owner = (1 - side) * 2 + slot if slot < 2 else 4
        spot = place(txt_refs, group, owner)
        return remote(spot, spot, pass_send.at[slot, group], gate_recv.at[slot, group], dp(partner))

    def pass_on(slot):
        for group in range(3):
            cross(slot, group).wait_recv()

            @pl.when(is_gate)
            def _():
                cross(slot, group).start()

    lanes = gacc[...]
    racc[0] = lanes[:, :HEAD_DIM] + lanes[:, HEAD_DIM:]

    def exchange(n):
        return [
            remote(racc.at[n], rbuf.at[n, j], red_send.at[n, j], red_recv.at[n, j], to)
            for j, to in enumerate(stages[n])
        ]

    for n in range(3):
        for c in exchange(n):
            c.start()
        if n < 2:
            pass_on(n)
        else:

            @pl.when(extra // 2 != side)
            def _():
                pass_on(2)

        for c in exchange(n):
            c.wait()
        value = racc[n]
        for j in range(7):
            value = value + rbuf[n, j]
        if n < 2:
            racc[n + 1] = value
        else:
            gain_out[...] = value

    def finish(t):
        for group in range(3):
            keep(t, group).wait()
            for i in (1, 2, 3):
                give(t, group, i).wait_send()
            gate, near, here = text_copies(t, group)
            gate.wait_send()
            near.wait_send()
            here.wait()

    def await_partner(t, owner):
        for group in range(3):
            spot = place(txt_refs, group, owner)
            remote(spot, spot, txt_send.at[t, group], txt_recv.at[t, group], dp(partner)).wait_recv()

    def await_given(t, i, owner):
        for group in range(3):
            spot = place(img_refs, group, owner)
            remote(
                spot, spot, out_send.at[t, group, i], out_recv.at[t, group, i], dp(source(i))
            ).wait_recv()

    finish(0)
    await_partner(0, partner)
    for i in (1, 2, 3):
        await_given(0, i, source(i))
        for a in range(4):
            hand(a, i).wait_send()

    @pl.when(me == extra)
    def _():
        finish(1)

    @pl.when(me != extra)
    def _():
        await_given(1, lax.rem(me + 4 - extra, 4), 4)
        for a in range(4):
            hand_extra(a).wait_send()

    @pl.when(partner == extra)
    def _():
        await_partner(1, 4)

    @pl.when(is_gate)
    def _():
        for slot in (0, 1):
            for group in range(3):
                cross(slot, group).wait_send()

    @pl.when(jnp.logical_and(is_gate, extra // 2 != side))
    def _():
        for group in range(3):
            cross(2, group).wait_send()


def local(iq, ik, iv, tq, tk, tv, ig, tg, gains):
    rows, width = iq.shape[1], iq.shape[2]
    anywhere = pl.BlockSpec(memory_space=pl.ANY)
    vmem = pl.BlockSpec(memory_space=pltpu.VMEM)
    dma = pltpu.SemaphoreType.DMA
    out = jax.ShapeDtypeStruct((1, rows, width), bf16)
    grads = jax.ShapeDtypeStruct((3, 1, rows, width), bf16)
    tall = (BLOCKS * ROWS, LANES)
    wide = (LANES, BLOCKS * ROWS)
    return pl.pallas_call(
        kernel,
        out_shape=(out, out, grads, grads, jax.ShapeDtypeStruct(gains.shape, f32)),
        in_specs=[anywhere] * 8 + [vmem],
        out_specs=(anywhere,) * 4 + (vmem,),
        scratch_shapes=[
            pltpu.VMEM((2, 4, *tall), bf16),
            pltpu.VMEM((2, 4, *tall), bf16),
            pltpu.VMEM(tall, bf16),
            pltpu.VMEM(tall, f32),
            pltpu.VMEM(tall, f32),
            pltpu.VMEM(wide, bf16),
            pltpu.VMEM(wide, bf16),
            pltpu.VMEM(tall, f32),
            pltpu.VMEM(tall, f32),
            pltpu.VMEM((4, LANES), f32),
            pltpu.VMEM((3, 4, HEAD_DIM), f32),
            pltpu.VMEM((3, 7, 4, HEAD_DIM), f32),
            dma((2, 4, 2)),
            dma((2, 4, 4)),
            dma((2, 4, 4)),
            dma((2, 3, 4)),
            dma((2, 3, 4)),
            dma((2, 3)),
            dma((2, 3)),
            dma((2, 3)),
            dma((2, 3)),
            dma((3, 3)),
            dma((3, 3)),
            dma((3, 7)),
            dma((3, 7)),
        ],
        compiler_params=pltpu.CompilerParams(
            collective_id=0, has_side_effects=True, vmem_limit_bytes=48 << 20
        ),
        name="joint_attention",
    )(iq, ik, iv, tq, tk, tv, ig, tg, gains)


def solution(mesh):
    image, text = P("seq", "dp", "tensor"), P("seq", None, "tensor")
    in_specs = (image, image, image, text, text, text, image, text, P())
    out_specs = (image, text, P(None, "seq", "dp", "tensor"), P(None, "seq", None, "tensor"), P())
    return jax.shard_map(local, mesh=mesh, in_specs=in_specs, out_specs=out_specs, check_vma=False)
```

time: 336 us -> 74.5 us (0.22)
  the two profiles are of different devices: /device:TPU:1 before, /device:TPU:2 now
where the time goes in v1:
time: 74.5 us; the launch traced here: 74.2 us
  Pallas kernels  62.1 us (83%)
  local copies, waits for them, and re-layouts  11.5 us (15%)
    pallas_call x1, Pallas kernels, local(): pl.pallas_call(kernel, out_shape=(out, out, grads, grads, jax.ShapeDtypeS...  62.1 us
    unnamed x23, local copies, waits for them, and re-layouts  11.5 us

profile of v1, /device:TPU:2, one launch (start us, length us, event | category | flops | bytes accessed | tf_op | source)
XLA Modules:
  0.0 74.2 jit_solution(4046524436186116957)
XLA Ops:
  0.6 0.0 copy-start
  0.6 0.9 %copy-done = bf16[1,128,640]{2,1,0:T(8,128)(2,1)S(1)} copy-done((bf16[1,128,640]{2,1,0:T(8,128)(2,1)S(1)}, bf16[1,128,640]{2,1,0:T(8,128)(2,1)}, u32[]{:S(2)}) %copy-start) | copy-done | bytes 163864
  1.6 0.0 copy-start.1
  1.6 0.9 %copy-done.1 = bf16[1,128,640]{2,1,0:T(8,128)(2,1)S(1)} copy-done((bf16[1,128,640]{2,1,0:T(8,128)(2,1)S(1)}, bf16[1,128,640]{2,1,0:T(8,128)(2,1)}, u32[]{:S(2)}) %copy-start.1) | copy-done | bytes 163864
  2.5 0.0 copy-start.2
  2.5 0.9 %copy-done.2 = bf16[1,128,640]{2,1,0:T(8,128)(2,1)S(1)} copy-done((bf16[1,128,640]{2,1,0:T(8,128)(2,1)S(1)}, bf16[1,128,640]{2,1,0:T(8,128)(2,1)}, u32[]{:S(2)}) %copy-start.2) | copy-done | bytes 163864
  3.4 0.0 copy-start.3
  3.4 0.9 %copy-done.3 = bf16[1,128,640]{2,1,0:T(8,128)(2,1)S(1)} copy-done((bf16[1,128,640]{2,1,0:T(8,128)(2,1)S(1)}, bf16[1,128,640]{2,1,0:T(8,128)(2,1)}, u32[]{:S(2)}) %copy-start.3) | copy-done | bytes 163864
  4.3 0.0 copy-start.4
  4.3 0.9 %copy-done.4 = bf16[1,128,640]{2,1,0:T(8,128)(2,1)S(1)} copy-done((bf16[1,128,640]{2,1,0:T(8,128)(2,1)S(1)}, bf16[1,128,640]{2,1,0:T(8,128)(2,1)}, u32[]{:S(2)}) %copy-start.4) | copy-done | bytes 163864
  5.2 0.0 copy-start.5
  5.2 0.9 %copy-done.5 = bf16[1,128,640]{2,1,0:T(8,128)(2,1)S(1)} copy-done((bf16[1,128,640]{2,1,0:T(8,128)(2,1)S(1)}, bf16[1,128,640]{2,1,0:T(8,128)(2,1)}, u32[]{:S(2)}) %copy-start.5) | copy-done | bytes 163864
  6.1 0.0 copy-start.6
  6.1 0.9 %copy-done.6 = bf16[1,128,640]{2,1,0:T(8,128)(2,1)S(1)} copy-done((bf16[1,128,640]{2,1,0:T(8,128)(2,1)S(1)}, bf16[1,128,640]{2,1,0:T(8,128)(2,1)}, u32[]{:S(2)}) %copy-start.6) | copy-done | bytes 163864
  7.0 0.0 copy-start.7
  7.1 0.9 %copy-done.7 = bf16[1,128,640]{2,1,0:T(8,128)(2,1)S(1)} copy-done((bf16[1,128,640]{2,1,0:T(8,128)(2,1)S(1)}, bf16[1,128,640]{2,1,0:T(8,128)(2,1)}, u32[]{:S(2)}) %copy-start.7) | copy-done | bytes 163864
  8.0 0.0 copy-start.8
  8.0 0.7 copy-done.8
  8.6 62.1 %joint_attention.1 = (bf16[1,128,640]{2,1,0:T(8,128)(2,1)S(1)}, bf16[1,128,640]{2,1,0:T(8,128)(2,1)S(1)}, bf16[3,1,128,640]{3,2,1,0:T(8,128)(2,1)S(1)}, bf16[3,1,128,640]{3,2,1,0:T(8,128)(2,1)S(1)}, f32[4,64]{1,0:T(4,128)S(1)}) custom-call(bf16[1,128,640]{2,1,0:T(8,128)(2,1)S(1)} %copy-done, bf16[1,128,640]{2,1,0:T(8,128)(2,1)S(1)} %copy-done.1, ...), custom_call_target="tpu_custom_call" | custom-call | tf_op jit(solution)/shard_map/joint_attention/pallas_call | solution.py:421
  70.7 0.7 copy.19
  71.4 0.7 copy.20
  72.1 0.8 %copy.21 = bf16[3,1,128,640]{3,2,1,0:T(8,128)(2,1)} copy(bf16[3,1,128,640]{3,2,1,0:T(8,128)(2,1)S(1)} %get-tuple-element.12) | data formatting | bytes 983040
  72.9 0.8 %copy.22 = bf16[3,1,128,640]{3,2,1,0:T(8,128)(2,1)} copy(bf16[3,1,128,640]{3,2,1,0:T(8,128)(2,1)S(1)} %get-tuple-element.13) | data formatting | bytes 983040
  73.6 0.6 copy.23
Async XLA Ops:
  0.6 0.9 %copy-start = (bf16[1,128,640]{2,1,0:T(8,128)(2,1)S(1)}, bf16[1,128,640]{2,1,0:T(8,128)(2,1)}, u32[]{:S(2)}) copy-start(bf16[1,128,640]{2,1,0:T(8,128)(2,1)} %iq.1) | copy-start | bytes 491524
  1.6 0.9 %copy-start.1 = (bf16[1,128,640]{2,1,0:T(8,128)(2,1)S(1)}, bf16[1,128,640]{2,1,0:T(8,128)(2,1)}, u32[]{:S(2)}) copy-start(bf16[1,128,640]{2,1,0:T(8,128)(2,1)} %ik.1) | copy-start | bytes 491524
  2.5 0.9 %copy-start.2 = (bf16[1,128,640]{2,1,0:T(8,128)(2,1)S(1)}, bf16[1,128,640]{2,1,0:T(8,128)(2,1)}, u32[]{:S(2)}) copy-start(bf16[1,128,640]{2,1,0:T(8,128)(2,1)} %iv.1) | copy-start | bytes 491524
  3.4 0.9 %copy-start.3 = (bf16[1,128,640]{2,1,0:T(8,128)(2,1)S(1)}, bf16[1,128,640]{2,1,0:T(8,128)(2,1)}, u32[]{:S(2)}) copy-start(bf16[1,128,640]{2,1,0:T(8,128)(2,1)} %tq.1) | copy-start | bytes 491524
  4.3 0.9 %copy-start.4 = (bf16[1,128,640]{2,1,0:T(8,128)(2,1)S(1)}, bf16[1,128,640]{2,1,0:T(8,128)(2,1)}, u32[]{:S(2)}) copy-start(bf16[1,128,640]{2,1,0:T(8,128)(2,1)} %tk.1) | copy-start | bytes 491524
  5.2 0.9 %copy-start.5 = (bf16[1,128,640]{2,1,0:T(8,128)(2,1)S(1)}, bf16[1,128,640]{2,1,0:T(8,128)(2,1)}, u32[]{:S(2)}) copy-start(bf16[1,128,640]{2,1,0:T(8,128)(2,1)} %tv.1) | copy-start | bytes 491524
  6.1 0.9 %copy-start.6 = (bf16[1,128,640]{2,1,0:T(8,128)(2,1)S(1)}, bf16[1,128,640]{2,1,0:T(8,128)(2,1)}, u32[]{:S(2)}) copy-start(bf16[1,128,640]{2,1,0:T(8,128)(2,1)} %ig.1) | copy-start | bytes 491524
  7.0 0.9 %copy-start.7 = (bf16[1,128,640]{2,1,0:T(8,128)(2,1)S(1)}, bf16[1,128,640]{2,1,0:T(8,128)(2,1)}, u32[]{:S(2)}) copy-start(bf16[1,128,640]{2,1,0:T(8,128)(2,1)} %tg.1) | copy-start | bytes 491524
  8.0 0.7 copy-start.8

commit v2 on v1

--- a/solution.py
+++ b/solution.py
@@ -26,7 +26,7 @@
 
 
 def first_head():
-    return lax.broadcasted_iota(jnp.int32, (ROWS, LANES), 1) < HEAD_DIM
+    return lax.broadcasted_iota(jnp.int32, (BLOCKS * ROWS, LANES), 1) < HEAD_DIM
 
 
 def same_head():
@@ -63,21 +63,25 @@
 
 
 def own_blocks(x):
-    return jnp.concatenate([x[:HEAD_DIM, :ROWS], x[HEAD_DIM:, ROWS:]], axis=0)
-
-
-def prepare_keys(rows, ins, gain, nk, uk, rk):
-    u, r = norm(ins[1, rows, :].astype(f32), same_head())
-    uk[rows, :] = u
-    rk[rows, :] = r
-    nk[rows, :] = (u * gain).astype(bf16)
-
-
-def query_block(first_block, rows, ins, gain, nk, kt, vt, dk, dv, outs):
+    return jnp.concatenate([x[:HEAD_DIM, : BLOCKS * ROWS], x[HEAD_DIM:, BLOCKS * ROWS :]], axis=0)
+
+
+def prepare_keys(ins, gain, nk, uk, rk, kt, vt):
+    u, r = norm(ins[1].astype(f32), same_head())
+    uk[...] = u
+    rk[...] = r
+    n = (u * gain).astype(bf16)
+    nk[...] = n
+    eye = identity()
+    kt[...] = dot_nt(eye, n).astype(bf16)
+    vt[...] = dot_nt(eye, ins[2]).astype(bf16)
+
+
+def query_pass(ins, gain, nk, kt, vt, dk, dv, outs):
     same, first, eye = same_head(), first_head(), identity()
-    u, r = norm(ins[0, rows, :].astype(f32), same)
+    u, r = norm(ins[0].astype(f32), same)
     q = by_head((u * gain).astype(bf16), first)
-    cot = ins[3, rows, :]
+    cot = ins[3]
     g = by_head(cot, first)
     s = dot_nt(nk[...], q)
     e = jnp.exp2(s * (LOG2E * HEAD_DIM**-0.5))
@@ -85,7 +89,9 @@
     p = e * (1.0 / total)
     pb = p.astype(bf16)
     out_t = own_blocks(dot(vt[...], pb)).astype(bf16)
-    outs[0, rows, :] = dot_nt(eye, out_t).astype(bf16)
+    for b in range(BLOCKS):
+        rows = slice(b * ROWS, (b + 1) * ROWS)
+        outs[0, rows, :] = dot_nt(eye, out_t[:, rows]).astype(bf16)
     z = out_t.astype(f32) * dot_nt(eye, cot)
     delta = jnp.concatenate(
         [
@@ -95,33 +101,32 @@
         axis=1,
     )
     ds = (p * (dot_nt(ins[2], g) - delta)).astype(bf16)
-    new_dk, new_dv = dot(ds, q), dot(pb, g)
-    if first_block:
-        dk[...] = new_dk
-        dv[...] = new_dv
-    else:
-        dk[...] += new_dk
-        dv[...] += new_dv
+    dk[...] = dot(ds, q)
+    dv[...] = dot(pb, g)
     y = jnp.transpose(own_blocks(dot(kt[...], ds))) * HEAD_DIM**-0.5
-    outs[1, rows, :] = norm_back(y, u, r, gain, same)
-    return jnp.sum(y * u, axis=0, keepdims=True)
-
-
-def key_block(rows, gain, dk, dv, uk, rk, outs):
-    y = dk[rows, :] * HEAD_DIM**-0.5
-    u, r = uk[rows, :], rk[rows, :]
-    outs[2, rows, :] = norm_back(y, u, r, gain, same_head())
-    outs[3, rows, :] = dv[rows, :].astype(bf16)
-    return jnp.sum(y * u, axis=0, keepdims=True)
+    outs[1] = norm_back(y, u, r, gain, same)
+    return y * u
+
+
+def key_pass(gain, dk, dv, uk, rk, outs):
+    y = dk[...] * HEAD_DIM**-0.5
+    u, r = uk[...], rk[...]
+    outs[2] = norm_back(y, u, r, gain, same_head())
+    outs[3] = dv[...].astype(bf16)
+    return y * u
+
+
+def image_and_text(x):
+    return [jnp.sum(x[:TEXT], axis=0, keepdims=True), jnp.sum(x[TEXT:], axis=0, keepdims=True)]
 
 
 def kernel(
     iq, ik, iv, tq, tk, tv, ig, tg, gains_ref,
     img_out, txt_out, img_grads, txt_grads, gain_out,
-    inb, outb, nk, uk, rk, kt, vt, dk, dv, gacc, racc, rbuf,
+    inb, outb, gain_rows, nk, uk, rk, kt, vt, dk, dv, gacc, racc, rbuf,
     in_local, in_send, in_recv, out_send, out_recv,
     txt_local, txt_send, txt_recv, gate_send, gate_recv, pass_send,
-    red_send, red_recv,
+    red_send, red_recv, present,
 ):
     me = lax.axis_index("dp")
     seq = lax.axis_index("seq")
@@ -172,22 +177,43 @@
             for part in (1, 0):
                 load(1, a, part).start()
 
-    stages = (
-        [
-            (me, (lax.rem(x + i, 4) * 8 + z) * 2 + lax.rem(core + j, 2), tensor)
-            for i in range(4)
-            for j in range(2)
-            if i or j
-        ],
-        [(me, (x * 8 + lax.rem(z + i, 8)) * 2 + core, tensor) for i in range(1, 8)],
-        [(lax.rem(y + i, 4), seq, lax.rem(y + i, 8) // 4) for i in range(1, 8)],
-    )
-
+    def along_y(k):
+        return (lax.rem(k, 4), seq, k // 4)
+
+    def along_x(k):
+        return (me, (lax.rem(k, 4) * 8 + z) * 2 + k // 4, tensor)
+
+    def along_z(k):
+        return (me, (x * 8 + k) * 2 + core, tensor)
+
+    place_x = core * 4 + x
+    rings = ((y, along_y), (place_x, along_x), (z, along_z))
+    later = (4 * (1 - tensor), 7 - place_x, 7 - z)
     barrier = pltpu.get_barrier_semaphore()
-    for stage in stages:
-        for to in stage:
-            pl.semaphore_signal(barrier, inc=1, device_id=to, device_id_type=MESH)
-    pl.semaphore_wait(barrier, sum(len(stage) for stage in stages))
+
+    def greet(sem, to):
+        pl.semaphore_signal(sem, inc=1, device_id=to, device_id_type=MESH)
+
+    for i in (1, 2, 3):
+        greet(barrier, dp(peer(i)))
+
+    def each_pair(act, want_later):
+        @pl.when(tensor == (0 if want_later else 1))
+        def _():
+            for k in range(4):
+                act(0, (k, seq, 1 - tensor))
+
+        for n in (1, 2):
+            mine, member = rings[n]
+            for k in range(8):
+                ahead = mine < k if want_later else mine > k
+
+                @pl.when(ahead)
+                def _():
+                    act(n, member(k))
+
+    each_pair(lambda n, to: greet(barrier, to), True)
+    pl.semaphore_wait(barrier, 3 + 4 * tensor + place_x + z)
 
     def hand(a, i):
         to = peer(i)
@@ -213,6 +239,8 @@
     def _():
         for a in (1, 2, 0, 3):
             hand_extra(a).start()
+
+    each_pair(lambda n, to: greet(present.at[n], to), False)
 
     def await_rows(t, a, j):
         if j == 0 or j == 1:
@@ -263,50 +291,78 @@
             pltpu.make_async_copy(rows, spot, txt_local.at[t, group]),
         )
 
-    gain = [jnp.concatenate([gains_ref[k : k + 1, :]] * 2, axis=1) for k in range(4)]
+    def send_text(t):
+        for group in range(3):
+            for c in text_copies(t, group):
+                c.start()
+
+    def send_images(t):
+        for group in range(3):
+            for i in (2, 3, 1):
+                give(t, group, i).start()
+            keep(t, group).start()
+
+    def exchange(n):
+        mine, member = rings[n]
+        return [
+            remote(
+                racc.at[n], rbuf.at[n, i], red_send.at[n, i], red_recv.at[n, i], member(lax.rem(mine + i, 8))
+            )
+            for i in range(1, 8)
+        ]
+
+    def start_exchange(n):
+        @pl.when(later[n] > 0)
+        def _():
+            pl.semaphore_wait(present.at[n], later[n])
+
+        for c in exchange(n):
+            c.start()
+
+    def start_sums():
+        lanes = gacc[...]
+        racc[0] = lanes[:, :HEAD_DIM] + lanes[:, HEAD_DIM:]
+        start_exchange(0)
+
+    pairs = jnp.concatenate([gains_ref[...]] * 2, axis=1)
+    is_text = lax.broadcasted_iota(jnp.int32, (BLOCKS * ROWS, LANES), 0) >= TEXT
+    for k in range(2):
+        gain_rows[k] = jnp.where(is_text, pairs[k + 2 : k + 3], pairs[k : k + 1])
     gacc[...] = jnp.zeros_like(gacc)
 
     def do_tile(t, carry):
         ins, outs = inb.at[t], outb.at[t]
 
-        def rows_of(j):
-            return pl.ds(TEXT, ROWS) if j == 0 else block(me) if j == 1 else block(source(j - 1))
-
-        def send(j, group):
-            if j == 0:
-                for c in text_copies(t, group):
-                    c.start()
-            elif j == 1:
-                keep(t, group).start()
-            else:
-                give(t, group, 5 - j).start()
-
-        for j in range(BLOCKS):
-            await_rows(t, 1, j)
-            prepare_keys(rows_of(j), ins, gain[3 if j == 0 else 1], nk, uk, rk)
-        for j in range(BLOCKS):
-            await_rows(t, 2, j)
-        eye = identity()
-        kt[...] = dot_nt(eye, nk[...]).astype(bf16)
-        vt[...] = dot_nt(eye, ins[2]).astype(bf16)
-        parts = []
-        for j in range(BLOCKS):
-            await_rows(t, 0, j)
-            await_rows(t, 3, j)
-            parts.append(
-                query_block(j == 0, rows_of(j), ins, gain[2 if j == 0 else 0], nk, kt, vt, dk, dv, outs)
-            )
-            send(j, 0)
-            send(j, 1)
-        key_parts = []
-        for j in range(BLOCKS):
-            key_parts.append(
-                key_block(rows_of(j), gain[3 if j == 0 else 1], dk, dv, uk, rk, outs)
-            )
-            send(j, 2)
-        gacc[...] += jnp.concatenate(
-            [sum(parts[1:]), sum(key_parts[1:]), parts[0], key_parts[0]], axis=0
-        )
+        for a in (1, 2):
+            for j in range(BLOCKS):
+                await_rows(t, a, j)
+        prepare_keys(ins, gain_rows[1], nk, uk, rk, kt, vt)
+        for a in (0, 3):
+            for j in range(BLOCKS):
+                await_rows(t, a, j)
+        query = image_and_text(query_pass(ins, gain_rows[0], nk, kt, vt, dk, dv, outs))
+        key = image_and_text(key_pass(gain_rows[1], dk, dv, uk, rk, outs))
+        gacc[...] += jnp.concatenate([query[0], key[0], query[1], key[1]], axis=0)
+
+        @pl.when(t == 0)
+        def _():
+            @pl.when(me != extra)
+            def _():
+                start_sums()
+
+            send_text(0)
+
+            @pl.when(me != extra)
+            def _():
+                send_images(0)
+
+        @pl.when(t == 1)
+        def _():
+            start_sums()
+            send_images(0)
+            send_text(1)
+            send_images(1)
+
         return carry
 
     lax.fori_loop(0, jnp.where(me == extra, 2, 1), do_tile, 0)
@@ -324,35 +380,24 @@
             def _():
                 cross(slot, group).start()
 
-    lanes = gacc[...]
-    racc[0] = lanes[:, :HEAD_DIM] + lanes[:, HEAD_DIM:]
-
-    def exchange(n):
-        return [
-            remote(racc.at[n], rbuf.at[n, j], red_send.at[n, j], red_recv.at[n, j], to)
-            for j, to in enumerate(stages[n])
-        ]
-
     for n in range(3):
-        for c in exchange(n):
-            c.start()
-        if n < 2:
-            pass_on(n)
-        else:
-
-            @pl.when(extra // 2 != side)
-            def _():
-                pass_on(2)
-
+        if n == 2:
+            pass_on(0)
+            pass_on(1)
         for c in exchange(n):
             c.wait()
         value = racc[n]
-        for j in range(7):
-            value = value + rbuf[n, j]
+        for i in range(1, 8):
+            value = value + rbuf[n, i]
         if n < 2:
             racc[n + 1] = value
+            start_exchange(n + 1)
         else:
             gain_out[...] = value
+
+    @pl.when(extra // 2 != side)
+    def _():
+        pass_on(2)
 
     def finish(t):
         for group in range(3):
@@ -409,23 +454,47 @@
             cross(2, group).wait_send()
 
 
+def store_kernel(a, b, c, d, e, oa, ob, oc, od, oe, sems):
+    copies = [
+        pltpu.make_async_copy(src, dst, sems.at[n])
+        for n, (src, dst) in enumerate(((a, oa), (b, ob), (c, oc), (d, od), (e, oe)))
+    ]
+    for copy in copies:
+        copy.start()
+    for copy in copies:
+        copy.wait()
+
+
+def store(results):
+    anywhere = pl.BlockSpec(memory_space=pl.ANY)
+    return pl.pallas_call(
+        store_kernel,
+        out_shape=tuple(jax.ShapeDtypeStruct(r.shape, r.dtype) for r in results),
+        in_specs=[pl.BlockSpec(memory_space=pltpu.VMEM)] * 5,
+        out_specs=(anywhere,) * 5,
+        scratch_shapes=[pltpu.SemaphoreType.DMA((5,))],
+        name="store_results",
+    )(*results)
+
+
 def local(iq, ik, iv, tq, tk, tv, ig, tg, gains):
     rows, width = iq.shape[1], iq.shape[2]
-    anywhere = pl.BlockSpec(memory_space=pl.ANY)
+    anywhere = pl.BlockSpec(memory_space=pltpu.HBM)
     vmem = pl.BlockSpec(memory_space=pltpu.VMEM)
     dma = pltpu.SemaphoreType.DMA
     out = jax.ShapeDtypeStruct((1, rows, width), bf16)
     grads = jax.ShapeDtypeStruct((3, 1, rows, width), bf16)
     tall = (BLOCKS * ROWS, LANES)
     wide = (LANES, BLOCKS * ROWS)
-    return pl.pallas_call(
+    return store(pl.pallas_call(
         kernel,
         out_shape=(out, out, grads, grads, jax.ShapeDtypeStruct(gains.shape, f32)),
         in_specs=[anywhere] * 8 + [vmem],
-        out_specs=(anywhere,) * 4 + (vmem,),
+        out_specs=(vmem,) * 5,
         scratch_shapes=[
             pltpu.VMEM((2, 4, *tall), bf16),
             pltpu.VMEM((2, 4, *tall), bf16),
+            pltpu.VMEM((2, *tall), f32),
             pltpu.VMEM(tall, bf16),
             pltpu.VMEM(tall, f32),
             pltpu.VMEM(tall, f32),
@@ -435,7 +504,7 @@
             pltpu.VMEM(tall, f32),
             pltpu.VMEM((4, LANES), f32),
             pltpu.VMEM((3, 4, HEAD_DIM), f32),
-            pltpu.VMEM((3, 7, 4, HEAD_DIM), f32),
+            pltpu.VMEM((3, 8, 4, HEAD_DIM), f32),
             dma((2, 4, 2)),
             dma((2, 4, 4)),
             dma((2, 4, 4)),
@@ -447,14 +516,15 @@
             dma((2, 3)),
             dma((3, 3)),
             dma((3, 3)),
-            dma((3, 7)),
-            dma((3, 7)),
+            dma((3, 8)),
+            dma((3, 8)),
+            pltpu.SemaphoreType.REGULAR((3,)),
         ],
         compiler_params=pltpu.CompilerParams(
-            collective_id=0, has_side_effects=True, vmem_limit_bytes=48 << 20
+            collective_id=0, has_side_effects=True, vmem_limit_bytes=63 << 20
         ),
         name="joint_attention",
-    )(iq, ik, iv, tq, tk, tv, ig, tg, gains)
+    )(iq, ik, iv, tq, tk, tv, ig, tg, gains))
 
 
 def solution(mesh):

time: 74.5 us -> 56.6 us (0.76)
  the two profiles are of different devices: /device:TPU:2 before, /device:TPU:1 now
where the time goes in v2:
time: 56.6 us; the launch traced here: 56.4 us
  Pallas kernels  55.8 us (99%)
  between operations  0.64 us (1%)
    pallas_call x1, Pallas kernels, local(): pl.pallas_call(kernel, out_shape=(out, out, grads, grads, jax.ShapeDtypeS...  53.3 us
    pallas_call x1, Pallas kernels, store(): pl.pallas_call(store_kernel, out_shape=tuple((jax.ShapeDtypeStruct(r.shap...  2.41 us

profile of v2, /device:TPU:1, one launch (start us, length us, event | category | flops | bytes accessed | tf_op | source)
XLA Modules:
  0.0 56.4 jit_solution(4090257480488581692)
XLA Ops:
  0.6 53.3 %joint_attention.1 = (bf16[1,128,640]{2,1,0:T(8,128)(2,1)}, bf16[1,128,640]{2,1,0:T(8,128)(2,1)}, bf16[3,1,128,640]{3,2,1,0:T(8,128)(2,1)}, bf16[3,1,128,640]{3,2,1,0:T(8,128)(2,1)}, f32[4,64]{1,0:T(4,128)}) custom-call(bf16[1,128,640]{2,1,0:T(8,128)(2,1)} %iq.1, bf16[1,128,640]{2,1,0:T(8,128)(2,1)} %ik.1, bf16[1,128,640]{2,1,0:T(8,128)(2,1)} %iv.1, ...), custom_call_target="tpu_custom_call" | custom-call | tf_op jit(solution)/shard_map/joint_attention/pallas_call | solution.py:489
  54.0 2.4 %store_results.1 = (bf16[1,128,640]{2,1,0:T(8,128)(2,1)}, bf16[1,128,640]{2,1,0:T(8,128)(2,1)}, bf16[3,1,128,640]{3,2,1,0:T(8,128)(2,1)}, bf16[3,1,128,640]{3,2,1,0:T(8,128)(2,1)}, f32[4,64]{1,0:T(4,128)}) custom-call(bf16[1,128,640]{2,1,0:T(8,128)(2,1)} %get-tuple-element.10.a, bf16[1,128,640]{2,1,0:T(8,128)(2,1)} %get-tuple-element.11.b, ...), custom_call_target="tpu_custom_call" | custom-call | tf_op jit(solution)/shard_map/store_results/pallas_call | solution.py:470

commit v3 on v2

v3 whole, which is shorter than its diff:
```python
import jax
import jax.numpy as jnp
from jax import lax
from jax.experimental import pallas as pl
from jax.experimental.pallas import tpu as pltpu
from jax.sharding import PartitionSpec as P

HEAD_DIM = 64
EPSILON = 1e-6
ROWS = 128
LANES = 128
BLOCKS = 5
TEXT = 4 * ROWS
LOG2E = 1.4426950408889634
MESH = pl.DeviceIdType.MESH
NT = (((1,), (1,)), ((), ()))
f32, bf16 = jnp.float32, jnp.bfloat16


def dot(a, b):
    return jnp.dot(a, b, preferred_element_type=f32)


def dot_nt(a, b):
    return lax.dot_general(a, b, NT, preferred_element_type=f32)


def first_head():
    return lax.broadcasted_iota(jnp.int32, (BLOCKS * ROWS, LANES), 1) < HEAD_DIM


def same_head():
    row = lax.broadcasted_iota(jnp.int32, (2 * LANES, LANES), 0)
    lane = lax.broadcasted_iota(jnp.int32, (2 * LANES, LANES), 1)
    return jnp.where(lax.rem(row, LANES) // HEAD_DIM == lane // HEAD_DIM, 1.0, 0.0).astype(bf16)


def identity():
    row = lax.broadcasted_iota(jnp.int32, (LANES, LANES), 0)
    lane = lax.broadcasted_iota(jnp.int32, (LANES, LANES), 1)
    return jnp.where(row == lane, 1.0, 0.0).astype(bf16)


def head_mean(z, same):
    high = z.astype(bf16)
    low = (z - high.astype(f32)).astype(bf16)
    return dot(jnp.concatenate([high, low], axis=1), same) * (1.0 / HEAD_DIM)


def norm(x, same):
    r = lax.rsqrt(head_mean(x * x, same) + EPSILON)
    return x * r, r


def norm_back(y, u, r, gain, same):
    w = y * gain
    return (r * (w - u * head_mean(w * u, same))).astype(bf16)


def by_head(x, first):
    zero = jnp.zeros_like(x)
    return jnp.concatenate([jnp.where(first, x, zero), jnp.where(first, zero, x)], axis=0)


def own_blocks(x):
    return jnp.concatenate([x[:HEAD_DIM, : BLOCKS * ROWS], x[HEAD_DIM:, BLOCKS * ROWS :]], axis=0)


def prepare_keys(ins, gain, nk, uk, rk, kt, vt):
    u, r = norm(ins[0].astype(f32), same_head())
    uk[...] = u
    rk[...] = r
    n = (u * gain).astype(bf16)
    nk[...] = n
    eye = identity()
    kt[...] = dot_nt(eye, n).astype(bf16)
    vt[...] = dot_nt(eye, ins[1]).astype(bf16)


def query_pass(ins, gain, nk, kt, vt, dk, dv, outs):
    same, first, eye = same_head(), first_head(), identity()
    u, r = norm(ins[2].astype(f32), same)
    q = by_head((u * gain).astype(bf16), first)
    cot = ins[3]
    g = by_head(cot, first)
    s = dot_nt(nk[...], q)
    e = jnp.exp2(s * (LOG2E * HEAD_DIM**-0.5))
    total = jnp.sum(e, axis=0, keepdims=True)
    p = e * (1.0 / total)
    pb = p.astype(bf16)
    out_t = own_blocks(dot(vt[...], pb)).astype(bf16)
    for b in range(BLOCKS):
        rows = slice(b * ROWS, (b + 1) * ROWS)
        outs[0, rows, :] = dot_nt(eye, out_t[:, rows]).astype(bf16)
    z = out_t.astype(f32) * dot_nt(eye, cot)
    delta = jnp.concatenate(
        [
            jnp.sum(z[:HEAD_DIM], axis=0, keepdims=True),
            jnp.sum(z[HEAD_DIM:], axis=0, keepdims=True),
        ],
        axis=1,
    )
    ds = (p * (dot_nt(ins[1], g) - delta)).astype(bf16)
    dk[...] = dot(ds, q)
    dv[...] = dot(pb, g)
    y = jnp.transpose(own_blocks(dot(kt[...], ds))) * HEAD_DIM**-0.5
    outs[1] = norm_back(y, u, r, gain, same)
    return y * u


def key_pass(gain, dk, dv, uk, rk, outs):
    y = dk[...] * HEAD_DIM**-0.5
    u, r = uk[...], rk[...]
    outs[2] = norm_back(y, u, r, gain, same_head())
    outs[3] = dv[...].astype(bf16)
    return y * u


def image_and_text(x):
    return [jnp.sum(x[:TEXT], axis=0, keepdims=True), jnp.sum(x[TEXT:], axis=0, keepdims=True)]


def kernel(
    iq, ik, iv, tq, tk, tv, ig, tg, gains_ref,
    img_out, txt_out, img_grads, txt_grads, gain_out,
    inb, outb, gain_rows, nk, uk, rk, kt, vt, dk, dv, racc, rbuf,
    in_send, in_recv, kept, text_send, out_recv, cross_recv, pass_send, red_send, red_recv, present,
):
    me = lax.axis_index("dp")
    seq = lax.axis_index("seq")
    tensor = lax.axis_index("tensor")
    core, z, x = lax.rem(seq, 2), lax.rem(seq // 2, 8), seq // 16
    y = tensor * 4 + me
    side = me // 2
    partner = me + 1 - 2 * lax.rem(me, 2)
    far_gate = 2 - side
    is_gate = jnp.logical_or(me == 1, me == 2)
    extra = 3 * core
    images = (ik, iv, iq, ig)
    texts = (tk, tv, tq, tg)

    def columns(owner):
        return pl.ds(pl.multiple_of(owner * LANES, LANES), LANES)

    def block(index):
        return pl.ds(pl.multiple_of(index * ROWS, ROWS), ROWS)

    def peer(i):
        return lax.rem(me + i, 4)

    def dp(index):
        return (index, seq, tensor)

    def remote(src, dst, send, recv, to):
        return pltpu.make_async_remote_copy(
            src_ref=src, dst_ref=dst, send_sem=send, recv_sem=recv, device_id=to, device_id_type=MESH
        )

    def drain(like, sem):
        pltpu.make_async_copy(like, like, sem).wait()

    def load(t):
        owner = me if t == 0 else 4
        for a in range(4):
            for refs, rows in ((texts, pl.ds(TEXT, ROWS)), (images, block(me))):
                pltpu.make_async_copy(
                    refs[a].at[0, :, columns(owner)], inb.at[t, a, rows], in_recv.at[t, a // 2]
                ).start()

    def along_y(k):
        return (lax.rem(k, 4), seq, k // 4)

    def along_x(k):
        return (me, (lax.rem(k, 4) * 8 + z) * 2 + k // 4, tensor)

    def along_z(k):
        return (me, (x * 8 + k) * 2 + core, tensor)

    place_x = core * 4 + x
    rings = ((y, along_y), (place_x, along_x), (z, along_z))
    later = (4 * (1 - tensor), 7 - place_x, 7 - z)
    barrier = pltpu.get_barrier_semaphore()

    def greet(sem, to):
        pl.semaphore_signal(sem, inc=1, device_id=to, device_id_type=MESH)

    for i in (1, 2, 3):
        greet(barrier, dp(peer(i)))

    def each_pair(act, want_later):
        @pl.when(tensor == (0 if want_later else 1))
        def _():
            for k in range(4):
                act(0, (k, seq, 1 - tensor))

        for n in (1, 2):
            mine, member = rings[n]
            for k in range(8):
                ahead = mine < k if want_later else mine > k

                @pl.when(ahead)
                def _():
                    act(n, member(k))

    each_pair(lambda n, to: greet(barrier, to), True)
    load(0)

    @pl.when(me == extra)
    def _():
        load(1)

    pl.semaphore_wait(barrier, 3 + 4 * tensor + place_x + z)

    def hand(a, i):
        to = peer(i)
        remote(
            images[a].at[0, :, columns(to)], inb.at[0, a, block(me)],
            in_send.at[0], in_recv.at[0, a // 2], dp(to),
        ).start()

    for pair in ((0, 1), (2, 3)):
        for i in (2, 3, 1):
            for a in pair:
                hand(a, i)

    @pl.when(me != extra)
    def _():
        for a in range(4):
            remote(
                images[a].at[0, :, columns(4)], inb.at[1, a, block(me)],
                in_send.at[1], in_recv.at[1, a // 2], dp(extra),
            ).start()

    each_pair(lambda n, to: greet(present.at[n], to), False)

    def result(t, group, rows):
        return outb.at[t, pl.ds(2, 2), rows] if group == 2 else outb.at[t, group, rows]

    def place(refs, group, owner):
        if group == 0:
            return refs[0].at[0, :, columns(owner)]
        if group == 1:
            return refs[1].at[0, 0, :, columns(owner)]
        return refs[1].at[pl.ds(1, 2), 0, :, columns(owner)]

    img_refs, txt_refs = (img_out, img_grads), (txt_out, txt_grads)

    def owner_of(t):
        return jnp.where(t == 0, me, 4)

    def send_text(t):
        for group in range(3):
            rows = result(t, group, pl.ds(TEXT, ROWS))
            spot = place(txt_refs, group, owner_of(t))
            remote(rows, spot, text_send.at[t], cross_recv.at[t], dp(far_gate)).start()
            remote(rows, spot, text_send.at[t], out_recv.at[2 * t], dp(partner)).start()
            pltpu.make_async_copy(rows, spot, kept.at[t]).start()

    def send_images(t):
        for group in range(3):
            spot = place(img_refs, group, owner_of(t))
            for i in (2, 3, 1):
                to = peer(i)
                remote(result(t, group, block(to)), spot, kept.at[t], out_recv.at[t], dp(to)).start()
            pltpu.make_async_copy(result(t, group, block(me)), spot, kept.at[t]).start()

    def start_exchange(n):
        @pl.when(later[n] > 0)
        def _():
            pl.semaphore_wait(present.at[n], later[n])

        mine, member = rings[n]
        for i in range(1, 8):
            remote(
                racc.at[n], rbuf.at[n, i], red_send.at[n], red_recv.at[n], member(lax.rem(mine + i, 8))
            ).start()

    pairs = jnp.concatenate([gains_ref[...]] * 2, axis=1)
    is_text = lax.broadcasted_iota(jnp.int32, (BLOCKS * ROWS, LANES), 0) >= TEXT
    for k in range(2):
        gain_rows[k] = jnp.where(is_text, pairs[k + 2 : k + 3], pairs[k : k + 1])
    racc[0] = jnp.zeros((4, LANES), f32)

    def do_tile(t, carry):
        ins, outs = inb.at[t], outb.at[t]
        drain(inb.at[t, pl.ds(0, 2)], in_recv.at[t, 0])
        prepare_keys(ins, gain_rows[1], nk, uk, rk, kt, vt)
        drain(inb.at[t, pl.ds(2, 2)], in_recv.at[t, 1])
        query = image_and_text(query_pass(ins, gain_rows[0], nk, kt, vt, dk, dv, outs))
        key = image_and_text(key_pass(gain_rows[1], dk, dv, uk, rk, outs))
        racc[0] += jnp.concatenate([query[0], key[0], query[1], key[1]], axis=0)

        @pl.when(t == 0)
        def _():
            @pl.when(me != extra)
            def _():
                start_exchange(0)

            send_text(0)

            @pl.when(me != extra)
            def _():
                send_images(0)

        @pl.when(t == 1)
        def _():
            start_exchange(0)
            send_images(0)
            send_text(1)
            send_images(1)

        return carry

    lax.fori_loop(0, jnp.where(me == extra, 2, 1), do_tile, 0)

    def pass_on(t):
        owners = [4] if t else [(1 - side) * 2, (1 - side) * 2 + 1]
        drain(outb.at[t, :, pl.ds(0, ROWS * len(owners))], cross_recv.at[t])

        @pl.when(is_gate)
        def _():
            for group in range(3):
                for owner in owners:
                    spot = place(txt_refs, group, owner)
                    remote(spot, spot, pass_send.at[t], cross_recv.at[t], dp(partner)).start()

    for n in range(3):
        if n == 2:
            pass_on(0)
        drain(rbuf.at[n, pl.ds(1, 7)], red_send.at[n])
        drain(rbuf.at[n, pl.ds(1, 7)], red_recv.at[n])
        value = racc[n]
        for i in range(1, 8):
            value = value + rbuf[n, i]
        if n < 2:
            racc[n + 1] = value
            start_exchange(n + 1)
        else:
            gain_out[...] = value[:, :HEAD_DIM] + value[:, HEAD_DIM:]

    @pl.when(extra // 2 != side)
    def _():
        pass_on(1)

    def finish(t):
        drain(outb.at[t], kept.at[t])
        drain(outb.at[t, :, pl.ds(0, 2 * ROWS)], text_send.at[t])

    finish(0)
    drain(outb.at[0, :, pl.ds(0, 4 * ROWS)], out_recv.at[0])
    drain(inb.at[0, :, pl.ds(0, 3 * ROWS)], in_send.at[0])

    @pl.when(me == extra)
    def _():
        finish(1)

    @pl.when(me != extra)
    def _():
        drain(outb.at[0, :, pl.ds(0, ROWS)], out_recv.at[1])
        drain(inb.at[0, :, pl.ds(0, ROWS)], in_send.at[1])

    @pl.when(partner == extra)
    def _():
        drain(outb.at[0, :, pl.ds(0, ROWS)], out_recv.at[2])

    @pl.when(is_gate)
    def _():
        drain(outb.at[0, :, pl.ds(0, 2 * ROWS)], pass_send.at[0])

    @pl.when(jnp.logical_and(is_gate, extra // 2 != side))
    def _():
        drain(outb.at[0, :, pl.ds(0, ROWS)], pass_send.at[1])


def store_kernel(a, b, c, d, e, oa, ob, oc, od, oe, sems):
    copies = [
        pltpu.make_async_copy(src, dst, sems.at[n])
        for n, (src, dst) in enumerate(((a, oa), (b, ob), (c, oc), (d, od), (e, oe)))
    ]
    for copy in copies:
        copy.start()
    for copy in copies:
        copy.wait()


def store(results):
    anywhere = pl.BlockSpec(memory_space=pl.ANY)
    return pl.pallas_call(
        store_kernel,
        out_shape=tuple(jax.ShapeDtypeStruct(r.shape, r.dtype) for r in results),
        in_specs=[pl.BlockSpec(memory_space=pltpu.VMEM)] * 5,
        out_specs=(anywhere,) * 5,
        scratch_shapes=[pltpu.SemaphoreType.DMA((5,))],
        name="store_results",
    )(*results)


def local(iq, ik, iv, tq, tk, tv, ig, tg, gains):
    rows, width = iq.shape[1], iq.shape[2]
    anywhere = pl.BlockSpec(memory_space=pltpu.HBM)
    vmem = pl.BlockSpec(memory_space=pltpu.VMEM)
    dma = pltpu.SemaphoreType.DMA
    out = jax.ShapeDtypeStruct((1, rows, width), bf16)
    grads = jax.ShapeDtypeStruct((3, 1, rows, width), bf16)
    tall = (BLOCKS * ROWS, LANES)
    wide = (LANES, BLOCKS * ROWS)
    return store(pl.pallas_call(
        kernel,
        out_shape=(out, out, grads, grads, jax.ShapeDtypeStruct(gains.shape, f32)),
        in_specs=[anywhere] * 8 + [vmem],
        out_specs=(vmem,) * 5,
        scratch_shapes=[
            pltpu.VMEM((2, 4, *tall), bf16),
            pltpu.VMEM((2, 4, *tall), bf16),
            pltpu.VMEM((2, *tall), f32),
            pltpu.VMEM(tall, bf16),
            pltpu.VMEM(tall, f32),
            pltpu.VMEM(tall, f32),
            pltpu.VMEM(wide, bf16),
            pltpu.VMEM(wide, bf16),
            pltpu.VMEM(tall, f32),
            pltpu.VMEM(tall, f32),
            pltpu.VMEM((3, 4, LANES), f32),
            pltpu.VMEM((3, 8, 4, LANES), f32),
            dma((2,)),
            dma((2, 2)),
            dma((2,)),
            dma((2,)),
            dma((3,)),
            dma((2,)),
            dma((2,)),
            dma((3,)),
            dma((3,)),
            pltpu.SemaphoreType.REGULAR((3,)),
        ],
        compiler_params=pltpu.CompilerParams(
            collective_id=0, has_side_effects=True, vmem_limit_bytes=63 << 20
        ),
        name="joint_attention",
    )(iq, ik, iv, tq, tk, tv, ig, tg, gains))


def solution(mesh):
    image, text = P("seq", "dp", "tensor"), P("seq", None, "tensor")
    in_specs = (image, image, image, text, text, text, image, text, P())
    out_specs = (image, text, P(None, "seq", "dp", "tensor"), P(None, "seq", None, "tensor"), P())
    return jax.shard_map(local, mesh=mesh, in_specs=in_specs, out_specs=out_specs, check_vma=False)
```

time: 56.6 us -> 54.7 us (0.966)
  Pallas kernels: 55.8 us -> 53.9 us
    pallas_call x1, Pallas kernels: 53.3 us -> 51.5 us  [local(): pl.pallas_call(kernel, out_shape=(out, out, grads, grads, jax.ShapeDtypeS...]
where the time goes in v3:
time: 54.7 us; the launch traced here: 54.5 us
  Pallas kernels  53.9 us (99%)
  between operations  0.64 us (1%)
    pallas_call x1, Pallas kernels, local(): pl.pallas_call(kernel, out_shape=(out, out, grads, grads, jax.ShapeDtypeS...  51.5 us
    pallas_call x1, Pallas kernels, store(): pl.pallas_call(store_kernel, out_shape=tuple((jax.ShapeDtypeStruct(r.shap...  2.41 us

profile of v3, /device:TPU:1, one launch (start us, length us, event | category | flops | bytes accessed | tf_op | source)
XLA Modules:
  0.0 54.5 jit_solution(4931687701038303161)
XLA Ops:
  0.6 51.5 %joint_attention.1 = (bf16[1,128,640]{2,1,0:T(8,128)(2,1)}, bf16[1,128,640]{2,1,0:T(8,128)(2,1)}, bf16[3,1,128,640]{3,2,1,0:T(8,128)(2,1)}, bf16[3,1,128,640]{3,2,1,0:T(8,128)(2,1)}, f32[4,64]{1,0:T(4,128)}) custom-call(bf16[1,128,640]{2,1,0:T(8,128)(2,1)} %iq.1, bf16[1,128,640]{2,1,0:T(8,128)(2,1)} %ik.1, bf16[1,128,640]{2,1,0:T(8,128)(2,1)} %iv.1, ...), custom_call_target="tpu_custom_call" | custom-call | tf_op jit(solution)/shard_map/joint_attention/pallas_call | solution.py:407
  52.1 2.4 %store_results.1 = (bf16[1,128,640]{2,1,0:T(8,128)(2,1)}, bf16[1,128,640]{2,1,0:T(8,128)(2,1)}, bf16[3,1,128,640]{3,2,1,0:T(8,128)(2,1)}, bf16[3,1,128,640]{3,2,1,0:T(8,128)(2,1)}, f32[4,64]{1,0:T(4,128)}) custom-call(bf16[1,128,640]{2,1,0:T(8,128)(2,1)} %get-tuple-element.10.a, bf16[1,128,640]{2,1,0:T(8,128)(2,1)} %get-tuple-element.11.b, ...), custom_call_target="tpu_custom_call" | custom-call | tf_op jit(solution)/shard_map/store_results/pallas_call | solution.py:388

commit v4 on v3

--- a/solution.py
+++ b/solution.py
@@ -77,7 +77,7 @@
     vt[...] = dot_nt(eye, ins[1]).astype(bf16)
 
 
-def query_pass(ins, gain, nk, kt, vt, dk, dv, outs):
+def query_pass(ins, gain, nk, kt, vt, dk, dv, outs, send_output):
     same, first, eye = same_head(), first_head(), identity()
     u, r = norm(ins[2].astype(f32), same)
     q = by_head((u * gain).astype(bf16), first)
@@ -92,6 +92,7 @@
     for b in range(BLOCKS):
         rows = slice(b * ROWS, (b + 1) * ROWS)
         outs[0, rows, :] = dot_nt(eye, out_t[:, rows]).astype(bf16)
+    send_output()
     z = out_t.astype(f32) * dot_nt(eye, cot)
     delta = jnp.concatenate(
         [
@@ -124,7 +125,7 @@
     iq, ik, iv, tq, tk, tv, ig, tg, gains_ref,
     img_out, txt_out, img_grads, txt_grads, gain_out,
     inb, outb, gain_rows, nk, uk, rk, kt, vt, dk, dv, racc, rbuf,
-    in_send, in_recv, kept, text_send, out_recv, cross_recv, pass_send, red_send, red_recv, present,
+    in_send, in_recv, kept, text_send, out_recv, cross_recv, pass_send, red_send, red_recv, total_send, total_recv, present,
 ):
     me = lax.axis_index("dp")
     seq = lax.axis_index("seq")
@@ -193,14 +194,16 @@
             for k in range(4):
                 act(0, (k, seq, 1 - tensor))
 
-        for n in (1, 2):
-            mine, member = rings[n]
-            for k in range(8):
-                ahead = mine < k if want_later else mine > k
-
-                @pl.when(ahead)
-                def _():
-                    act(n, member(k))
+        @pl.when(jnp.logical_not(is_gate))
+        def _():
+            for n in (1, 2):
+                mine, member = rings[n]
+                for k in range(8):
+                    ahead = mine < k if want_later else mine > k
+
+                    @pl.when(ahead)
+                    def _():
+                        act(n, member(k))
 
     each_pair(lambda n, to: greet(barrier, to), True)
     load(0)
@@ -209,7 +212,7 @@
     def _():
         load(1)
 
-    pl.semaphore_wait(barrier, 3 + 4 * tensor + place_x + z)
+    pl.semaphore_wait(barrier, 3 + 4 * tensor + jnp.where(is_gate, 0, place_x + z))
 
     def hand(a, i):
         to = peer(i)
@@ -248,16 +251,16 @@
     def owner_of(t):
         return jnp.where(t == 0, me, 4)
 
-    def send_text(t):
-        for group in range(3):
+    def send_text(t, groups):
+        for group in groups:
             rows = result(t, group, pl.ds(TEXT, ROWS))
             spot = place(txt_refs, group, owner_of(t))
             remote(rows, spot, text_send.at[t], cross_recv.at[t], dp(far_gate)).start()
             remote(rows, spot, text_send.at[t], out_recv.at[2 * t], dp(partner)).start()
             pltpu.make_async_copy(rows, spot, kept.at[t]).start()
 
-    def send_images(t):
-        for group in range(3):
+    def send_images(t, groups):
+        for group in groups:
             spot = place(img_refs, group, owner_of(t))
             for i in (2, 3, 1):
                 to = peer(i)
@@ -283,10 +286,16 @@
 
     def do_tile(t, carry):
         ins, outs = inb.at[t], outb.at[t]
+
+        def send_output():
+            @pl.when(jnp.logical_and(t == 0, me != extra))
+            def _():
+                send_text(0, (0,))
+
         drain(inb.at[t, pl.ds(0, 2)], in_recv.at[t, 0])
         prepare_keys(ins, gain_rows[1], nk, uk, rk, kt, vt)
         drain(inb.at[t, pl.ds(2, 2)], in_recv.at[t, 1])
-        query = image_and_text(query_pass(ins, gain_rows[0], nk, kt, vt, dk, dv, outs))
+        query = image_and_text(query_pass(ins, gain_rows[0], nk, kt, vt, dk, dv, outs, send_output))
         key = image_and_text(key_pass(gain_rows[1], dk, dv, uk, rk, outs))
         racc[0] += jnp.concatenate([query[0], key[0], query[1], key[1]], axis=0)
 
@@ -296,18 +305,18 @@
             def _():
                 start_exchange(0)
 
-            send_text(0)
-
             @pl.when(me != extra)
             def _():
-                send_images(0)
+                send_text(0, (1, 2))
+                send_images(0, (0, 1, 2))
 
         @pl.when(t == 1)
         def _():
             start_exchange(0)
-            send_images(0)
-            send_text(1)
-            send_images(1)
+            send_text(0, (0, 1, 2))
+            send_text(1, (0, 1, 2))
+            send_images(0, (0, 1, 2))
+            send_images(1, (0, 1, 2))
 
         return carry
 
@@ -324,23 +333,47 @@
                     spot = place(txt_refs, group, owner)
                     remote(spot, spot, pass_send.at[t], cross_recv.at[t], dp(partner)).start()
 
-    for n in range(3):
-        if n == 2:
-            pass_on(0)
+    def total(gate):
+        return remote(racc.at[3], racc.at[3], total_send.at[gate - 1], total_recv.at[0], dp(gate))
+
+    def end_exchange(n):
         drain(rbuf.at[n, pl.ds(1, 7)], red_send.at[n])
         drain(rbuf.at[n, pl.ds(1, 7)], red_recv.at[n])
-        value = racc[n]
-        for i in range(1, 8):
-            value = value + rbuf[n, i]
-        if n < 2:
+
+    @pl.when(jnp.logical_not(is_gate))
+    def _():
+        for n in range(3):
+            end_exchange(n)
+            value = racc[n]
+            for i in range(1, 8):
+                value = value + rbuf[n, i]
             racc[n + 1] = value
-            start_exchange(n + 1)
-        else:
-            gain_out[...] = value[:, :HEAD_DIM] + value[:, HEAD_DIM:]
+            if n < 2:
+                start_exchange(n + 1)
+
+        @pl.when(me != extra)
+        def _():
+            for gate in (1, 2):
+                total(gate).start()
+
+    pass_on(0)
 
     @pl.when(extra // 2 != side)
     def _():
         pass_on(1)
+
+    @pl.when(is_gate)
+    def _():
+        end_exchange(0)
+        drain(racc.at[3], total_recv.at[0])
+
+    @pl.when(jnp.logical_and(jnp.logical_not(is_gate), me != extra))
+    def _():
+        for gate in (1, 2):
+            total(gate).wait_send()
+
+    value = racc[3]
+    gain_out[...] = value[:, :HEAD_DIM] + value[:, HEAD_DIM:]
 
     def finish(t):
         drain(outb.at[t], kept.at[t])
@@ -372,25 +405,36 @@
         drain(outb.at[0, :, pl.ds(0, ROWS)], pass_send.at[1])
 
 
-def store_kernel(a, b, c, d, e, oa, ob, oc, od, oe, sems):
-    copies = [
-        pltpu.make_async_copy(src, dst, sems.at[n])
-        for n, (src, dst) in enumerate(((a, oa), (b, ob), (c, oc), (d, od), (e, oe)))
-    ]
-    for copy in copies:
+def store_kernel(a, b, c, d, e, oa, ob, oc, od, oe, stage, small, read, write):
+    pieces = [(c.at[k, 0], oc.at[k, 0]) for k in range(3)] + [(d.at[k, 0], od.at[k, 0]) for k in range(3)]
+    pieces += [(a.at[0], oa.at[0]), (b.at[0], ob.at[0])]
+    steps = [(src, stage.at[n], dst) for n, (src, dst) in enumerate(pieces)] + [(e, small, oe)]
+    reads = [pltpu.make_async_copy(src, mid, read.at[n]) for n, (src, mid, dst) in enumerate(steps)]
+    writes = [pltpu.make_async_copy(mid, dst, write.at[n]) for n, (src, mid, dst) in enumerate(steps)]
+    for copy in reads:
         copy.start()
-    for copy in copies:
+    for copy, onward in zip(reads, writes):
+        copy.wait()
+        onward.start()
+    for copy in writes:
         copy.wait()
 
 
 def store(results):
     anywhere = pl.BlockSpec(memory_space=pl.ANY)
+    rows, width = results[0].shape[1:]
     return pl.pallas_call(
         store_kernel,
         out_shape=tuple(jax.ShapeDtypeStruct(r.shape, r.dtype) for r in results),
-        in_specs=[pl.BlockSpec(memory_space=pltpu.VMEM)] * 5,
+        in_specs=[anywhere] * 5,
         out_specs=(anywhere,) * 5,
-        scratch_shapes=[pltpu.SemaphoreType.DMA((5,))],
+        scratch_shapes=[
+            pltpu.VMEM((8, rows, width), bf16),
+            pltpu.VMEM(results[4].shape, f32),
+            pltpu.SemaphoreType.DMA((9,)),
+            pltpu.SemaphoreType.DMA((9,)),
+        ],
+        compiler_params=pltpu.CompilerParams(vmem_limit_bytes=63 << 20),
         name="store_results",
     )(*results)
 
@@ -408,7 +452,7 @@
         kernel,
         out_shape=(out, out, grads, grads, jax.ShapeDtypeStruct(gains.shape, f32)),
         in_specs=[anywhere] * 8 + [vmem],
-        out_specs=(vmem,) * 5,
+        out_specs=(anywhere,) * 4 + (vmem,),
         scratch_shapes=[
             pltpu.VMEM((2, 4, *tall), bf16),
             pltpu.VMEM((2, 4, *tall), bf16),
@@ -420,7 +464,7 @@
             pltpu.VMEM(wide, bf16),
             pltpu.VMEM(tall, f32),
             pltpu.VMEM(tall, f32),
-            pltpu.VMEM((3, 4, LANES), f32),
+            pltpu.VMEM((4, 4, LANES), f32),
             pltpu.VMEM((3, 8, 4, LANES), f32),
             dma((2,)),
             dma((2, 2)),
@@ -431,6 +475,8 @@
             dma((2,)),
             dma((3,)),
             dma((3,)),
+            dma((2,)),
+            dma((1,)),
             pltpu.SemaphoreType.REGULAR((3,)),
         ],
         compiler_params=pltpu.CompilerParams(

time: 54.7 us -> 52.6 us (0.962)
  Pallas kernels: 53.9 us -> 51.8 us
    pallas_call x1, Pallas kernels: 51.5 us -> 49.6 us  [local(): pl.pallas_call(kernel, out_shape=(out, out, grads, grads, jax.ShapeDtypeS...]
where the time goes in v4:
time: 52.6 us; the launch traced here: 52.4 us
  Pallas kernels  51.8 us (98%)
  between operations  0.64 us (1%)
    pallas_call x1, Pallas kernels, local(): pl.pallas_call(kernel, out_shape=(out, out, grads, grads, jax.ShapeDtypeS...  49.6 us
    pallas_call x1, Pallas kernels, store(): pl.pallas_call(store_kernel, out_shape=tuple((jax.ShapeDtypeStruct(r.shap...  2.23 us

profile of v4, /device:TPU:1, one launch (start us, length us, event | category | flops | bytes accessed | tf_op | source)
XLA Modules:
  0.0 52.4 jit_solution(16653535371651016337)
XLA Ops:
  0.6 49.6 %joint_attention.1 = (bf16[1,128,640]{2,1,0:T(8,128)(2,1)}, bf16[1,128,640]{2,1,0:T(8,128)(2,1)}, bf16[3,1,128,640]{3,2,1,0:T(8,128)(2,1)}, bf16[3,1,128,640]{3,2,1,0:T(8,128)(2,1)}, f32[4,64]{1,0:T(4,128)}) custom-call(bf16[1,128,640]{2,1,0:T(8,128)(2,1)} %iq.1, bf16[1,128,640]{2,1,0:T(8,128)(2,1)} %ik.1, bf16[1,128,640]{2,1,0:T(8,128)(2,1)} %iv.1, ...), custom_call_target="tpu_custom_call" | custom-call | tf_op jit(solution)/shard_map/joint_attention/pallas_call | solution.py:451
  50.2 2.2 %store_results.1 = (bf16[1,128,640]{2,1,0:T(8,128)(2,1)}, bf16[1,128,640]{2,1,0:T(8,128)(2,1)}, bf16[3,1,128,640]{3,2,1,0:T(8,128)(2,1)}, bf16[3,1,128,640]{3,2,1,0:T(8,128)(2,1)}, f32[4,64]{1,0:T(4,128)}) custom-call(bf16[1,128,640]{2,1,0:T(8,128)(2,1)} %get-tuple-element.10.a, bf16[1,128,640]{2,1,0:T(8,128)(2,1)} %get-tuple-element.11.b, ...), custom_call_target="tpu_custom_call" | custom-call | tf_op jit(solution)/shard_map/store_results/pallas_call | solution.py:426

commit v5 on v4

--- a/solution.py
+++ b/solution.py
@@ -125,7 +125,7 @@
     iq, ik, iv, tq, tk, tv, ig, tg, gains_ref,
     img_out, txt_out, img_grads, txt_grads, gain_out,
     inb, outb, gain_rows, nk, uk, rk, kt, vt, dk, dv, racc, rbuf,
-    in_send, in_recv, kept, text_send, out_recv, cross_recv, pass_send, red_send, red_recv, total_send, total_recv, present,
+    in_send, in_recv, kept, text_send, out_recv, cross_recv, pass_send, red_send, red_recv, total_send, present,
 ):
     me = lax.axis_index("dp")
     seq = lax.axis_index("seq")
@@ -136,7 +136,7 @@
     partner = me + 1 - 2 * lax.rem(me, 2)
     far_gate = 2 - side
     is_gate = jnp.logical_or(me == 1, me == 2)
-    extra = 3 * core
+    extra = 3 * jnp.where(tensor == 1, core, 1 - core)
     images = (ik, iv, iq, ig)
     texts = (tk, tv, tq, tg)
 
@@ -174,12 +174,15 @@
     def along_x(k):
         return (me, (lax.rem(k, 4) * 8 + z) * 2 + k // 4, tensor)
 
-    def along_z(k):
-        return (me, (x * 8 + k) * 2 + core, tensor)
+    def along_z(who, k):
+        return (who, (x * 8 + k) * 2 + core, tensor)
+
+    source = 3 - extra
+    is_source = me == source
 
     place_x = core * 4 + x
-    rings = ((y, along_y), (place_x, along_x), (z, along_z))
-    later = (4 * (1 - tensor), 7 - place_x, 7 - z)
+    rings = ((y, along_y), (place_x, along_x), (z, lambda k: along_z(me, k)))
+    later = (4 * (1 - tensor), 7 - place_x, (7 - z) * jnp.where(is_source, 3, 1))
     barrier = pltpu.get_barrier_semaphore()
 
     def greet(sem, to):
@@ -205,6 +208,20 @@
                     def _():
                         act(n, member(k))
 
+        for k in range(8):
+            ahead = z < k if want_later else z > k
+
+            @pl.when(jnp.logical_and(is_gate, ahead))
+            def _():
+                act(2, along_z(source, k))
+
+            if want_later:
+
+                @pl.when(jnp.logical_and(is_source, ahead))
+                def _():
+                    for gate in (1, 2):
+                        act(2, along_z(gate, k))
+
     each_pair(lambda n, to: greet(barrier, to), True)
     load(0)
 
@@ -212,7 +229,7 @@
     def _():
         load(1)
 
-    pl.semaphore_wait(barrier, 3 + 4 * tensor + jnp.where(is_gate, 0, place_x + z))
+    pl.semaphore_wait(barrier, 3 + 4 * tensor + jnp.where(is_gate, z, place_x + z * jnp.where(is_source, 3, 1)))
 
     def hand(a, i):
         to = peer(i)
@@ -332,9 +349,6 @@
                 for owner in owners:
                     spot = place(txt_refs, group, owner)
                     remote(spot, spot, pass_send.at[t], cross_recv.at[t], dp(partner)).start()
-
-    def total(gate):
-        return remote(racc.at[3], racc.at[3], total_send.at[gate - 1], total_recv.at[0], dp(gate))
 
     def end_exchange(n):
         drain(rbuf.at[n, pl.ds(1, 7)], red_send.at[n])
@@ -350,11 +364,17 @@
             racc[n + 1] = value
             if n < 2:
                 start_exchange(n + 1)
-
-        @pl.when(me != extra)
-        def _():
-            for gate in (1, 2):
-                total(gate).start()
+            if n == 1:
+
+                @pl.when(is_source)
+                def _():
+                    for gate in (1, 2):
+                        for i in range(8):
+                            remote(
+                                racc.at[2], rbuf.at[2, i], total_send.at[0], red_recv.at[2],
+                                along_z(gate, lax.rem(z + i, 8)),
+                            ).start()
+
 
     pass_on(0)
 
@@ -365,12 +385,15 @@
     @pl.when(is_gate)
     def _():
         end_exchange(0)
-        drain(racc.at[3], total_recv.at[0])
-
-    @pl.when(jnp.logical_and(jnp.logical_not(is_gate), me != extra))
-    def _():
-        for gate in (1, 2):
-            total(gate).wait_send()
+        drain(rbuf.at[2], red_recv.at[2])
+        value = rbuf[2, 0]
+        for i in range(1, 8):
+            value = value + rbuf[2, i]
+        racc[3] = value
+
+    @pl.when(is_source)
+    def _():
+        drain(rbuf.at[pl.ds(0, 2)], total_send.at[0])
 
     value = racc[3]
     gain_out[...] = value[:, :HEAD_DIM] + value[:, HEAD_DIM:]
@@ -475,7 +498,6 @@
             dma((2,)),
             dma((3,)),
             dma((3,)),
-            dma((2,)),
             dma((1,)),
             pltpu.SemaphoreType.REGULAR((3,)),
         ],

time: 52.6 us -> 51.7 us (0.983)
  Pallas kernels: 51.8 us -> 50.9 us
    pallas_call x1, Pallas kernels: 49.6 us -> 48.7 us  [local(): pl.pallas_call(kernel, out_shape=(out, out, grads, grads, jax.ShapeDtypeS...]
where the time goes in v5:
time: 51.7 us; the launch traced here: 51.6 us
  Pallas kernels  50.9 us (98%)
  between operations  0.64 us (1%)
    pallas_call x1, Pallas kernels, local(): pl.pallas_call(kernel, out_shape=(out, out, grads, grads, jax.ShapeDtypeS...  48.7 us
    pallas_call x1, Pallas kernels, store(): pl.pallas_call(store_kernel, out_shape=tuple((jax.ShapeDtypeStruct(r.shap...  2.23 us

profile of v5, /device:TPU:1, one launch (start us, length us, event | category | flops | bytes accessed | tf_op | source)
XLA Modules:
  0.0 51.6 jit_solution(1570126456806979875)
XLA Ops:
  0.6 48.7 %joint_attention.1 = (bf16[1,128,640]{2,1,0:T(8,128)(2,1)}, bf16[1,128,640]{2,1,0:T(8,128)(2,1)}, bf16[3,1,128,640]{3,2,1,0:T(8,128)(2,1)}, bf16[3,1,128,640]{3,2,1,0:T(8,128)(2,1)}, f32[4,64]{1,0:T(4,128)}) custom-call(bf16[1,128,640]{2,1,0:T(8,128)(2,1)} %iq.1, bf16[1,128,640]{2,1,0:T(8,128)(2,1)} %ik.1, bf16[1,128,640]{2,1,0:T(8,128)(2,1)} %iv.1, ...), custom_call_target="tpu_custom_call" | custom-call | tf_op jit(solution)/shard_map/joint_attention/pallas_call | solution.py:474
  49.3 2.2 %store_results.1 = (bf16[1,128,640]{2,1,0:T(8,128)(2,1)}, bf16[1,128,640]{2,1,0:T(8,128)(2,1)}, bf16[3,1,128,640]{3,2,1,0:T(8,128)(2,1)}, bf16[3,1,128,640]{3,2,1,0:T(8,128)(2,1)}, f32[4,64]{1,0:T(4,128)}) custom-call(bf16[1,128,640]{2,1,0:T(8,128)(2,1)} %get-tuple-element.10.a, bf16[1,128,640]{2,1,0:T(8,128)(2,1)} %get-tuple-element.11.b, ...), custom_call_target="tpu_custom_call" | custom-call | tf_op jit(solution)/shard_map/store_results/pallas_call | solution.py:449
